TPU v7x, 256 devices: a whole 4x4x8 slice. The times are simulated.
256 devices in a mesh: kv: 64 (over y, z, core), tp: 4 (over x).
Axes of the slice: x: 4, y: 4, z: 8, core: 2. Of those that a mesh axis runs over, the one named last changes fastest.
Arguments:
- queries: bfloat16 [3, 512, 8192], P(None, ('kv', 'tp')), may hold values from -35 to 35
- new_keys: bfloat16 [3, 512, 1024], P(None, ('kv', 'tp')), may hold values from -6 to 6
- new_values: bfloat16 [3, 512, 1024], P(None, ('kv', 'tp')), may hold values from -6 to 6
- key_cache: bfloat16 [2560, 256, 1024], P('kv', None, 'tp'), may hold values from -21 to 21
- value_cache: bfloat16 [2560, 256, 1024], P('kv', None, 'tp'), may hold values from -6 to 6
- context_lengths: int32 [512], replicated, may hold values from 1 to 32768, as said below
- piece_slots: int32 [512, 128], replicated, may hold values from -1 to 2559, as said below
Outputs:
- attended: bfloat16 [3, 512, 8192], P(None, ('kv', 'tp'))
Inputs may be any that keep to these rules, and one draw needn't show every extreme that they name: Row b holds ceil(context_lengths[b] / 256) cache slots; some row holds 32768 tokens. piece_slots[b, p] is owner * 40 + local slot of the slot holding tokens p * 256 to (p + 1) * 256 - 1 of row b for p below ceil(context_lengths[b] / 256), and -1 after. Every slot holds exactly one piece. The slots of the 8 rows of one index of kv lie at most 3 times on one owner, and for some index of kv exactly 3 times on every owner.
All inputs are finite; a program needn't handle non-finite values.
Results may differ from a plain program's by a relative error of at most 0.0051.
Values may be sent and summed in bfloat16 or wider, within the bound.
A program may use at most 128 MiB of HBM per device.

v0:
```python
import math

import jax
import jax.numpy as jnp
from jax import lax
from jax.sharding import PartitionSpec as P

HD = 128


def slot_partials(slot_queries, key_cache, value_cache, counts, kv_local):
    steps, slots, width = slot_queries.shape
    group = width // (kv_local * HD)
    grid = slot_queries.reshape(steps, slots, kv_local, group, HD)
    keys = key_cache.reshape(slots, key_cache.shape[1], kv_local, HD)
    values = value_cache.reshape(slots, value_cache.shape[1], kv_local, HD)
    scores = jnp.einsum("tskgc,snkc->sktgn", grid, keys, preferred_element_type=jnp.float32) * (
        1.0 / math.sqrt(HD)
    )
    live = (
        jnp.arange(keys.shape[1], dtype=jnp.int32)[None, None, None, None, :]
        < counts[:, None, None, None, None]
    )
    scores = jnp.where(live, scores, -jnp.inf)
    top = jnp.max(scores, axis=-1)
    expo = jnp.exp(scores - top[..., None])
    total = jnp.sum(expo, axis=-1)
    weights = expo.astype(jnp.bfloat16)
    summed = jnp.einsum("sktgn,snkc->sktgc", weights, values, preferred_element_type=jnp.float32)
    return (top, total, (summed / total[..., None]).astype(jnp.bfloat16))


def shards(queries, new_keys, new_values, key_cache, value_cache, context_lengths, piece_slots):
    kv_count = lax.axis_size("kv")
    me = lax.axis_index("kv")
    q_mine, keys_mine, values_mine = (
        lax.all_to_all(queries, "tp", split_axis=2, concat_axis=1, tiled=True),
        lax.all_to_all(new_keys, "tp", split_axis=2, concat_axis=1, tiled=True),
        lax.all_to_all(new_values, "tp", split_axis=2, concat_axis=1, tiled=True),
    )
    steps, rows_group, width = q_mine.shape
    kv_local = keys_mine.shape[2] // HD
    group = width // keys_mine.shape[2]
    total_rows, pieces = piece_slots.shape
    slots_dev, slot_len = (key_cache.shape[0], key_cache.shape[1])
    capacity = (pieces + rows_group - 1 + kv_count - 1) // kv_count
    entries = kv_count * capacity
    group_len = rows_group * pieces
    used = piece_slots >= 0
    owners = jnp.where(used, piece_slots // slots_dev, kv_count)
    flat_grid = jnp.arange(total_rows * pieces, dtype=jnp.int32).reshape(total_rows, pieces)
    my_slots = me * slots_dev + jnp.arange(slots_dev, dtype=jnp.int32)
    holds = piece_slots[None, :, :] == my_slots[:, None, None]
    slot_flat = jnp.max(jnp.where(holds, flat_grid[None], -1), axis=(1, 2))
    slot_row = slot_flat // pieces
    slot_piece = slot_flat % pieces
    slot_group = slot_row // rows_group
    slot_local = slot_flat % group_len
    on_me = (owners == me).astype(jnp.float32).reshape(kv_count, group_len)
    group_pick = (slot_group[:, None] == jnp.arange(kv_count, dtype=jnp.int32)[None, :]).astype(
        jnp.float32
    )
    group_rows = jnp.dot(group_pick, on_me, precision=lax.Precision.HIGHEST)
    earlier = jnp.arange(group_len, dtype=jnp.int32)[None, :] < slot_local[:, None]
    slot_entry = jnp.sum(jnp.where(earlier, group_rows, 0.0), axis=1).astype(jnp.int32)
    row_pick = (slot_row[:, None] == jnp.arange(total_rows, dtype=jnp.int32)[None, :]).astype(
        jnp.int32
    )
    counts = jnp.minimum(
        slot_len, jnp.sum(row_pick * context_lengths[None, :], axis=1) - slot_piece * slot_len
    )
    slot_index = slot_group * capacity + slot_entry
    my_owners = lax.dynamic_slice_in_dim(owners, me * rows_group, rows_group, 0).reshape(-1)
    positions = jnp.arange(group_len, dtype=jnp.int32)
    same_owner = (my_owners[:, None] == my_owners[None, :]) & (
        positions[:, None] < positions[None, :]
    )
    my_rank = jnp.sum(same_owner.astype(jnp.int32), axis=0)
    local_row = positions // pieces
    cand = jnp.arange(entries, dtype=jnp.int32)
    matched = (my_owners[None, :] == (cand // capacity)[:, None]) & (
        my_rank[None, :] == (cand % capacity)[:, None]
    )
    entry_flat = jnp.max(jnp.where(matched, local_row[None, :], -1), axis=1)
    entry_live = entry_flat >= 0
    everyone = lax.all_gather(q_mine, "kv", axis=1, tiled=True)
    selector = row_pick.astype(jnp.bfloat16)
    slot_queries = jnp.einsum(
        "sb,tbw->tsw", selector, everyone, preferred_element_type=jnp.float32
    ).astype(jnp.bfloat16)
    top, total, out = slot_partials(slot_queries, key_cache, value_cache, counts, kv_local)
    placer = cand[:, None] == slot_index[None, :]
    placer_f = placer.astype(jnp.float32)
    top_send = jnp.einsum("es,sktg->ektg", placer_f, top, precision=lax.Precision.HIGHEST).reshape(
        (kv_count, capacity) + top.shape[1:]
    )
    total_send = jnp.einsum(
        "es,sktg->ektg", placer_f, total, precision=lax.Precision.HIGHEST
    ).reshape((kv_count, capacity) + total.shape[1:])
    out_send = jnp.einsum(
        "es,sktgc->ektgc", placer.astype(jnp.bfloat16), out, preferred_element_type=jnp.float32
    ).astype(jnp.bfloat16)
    out_send = out_send.reshape((kv_count, capacity) + out.shape[1:])
    out_back, top_back, total_back = (
        lax.all_to_all(
            out_send.astype(jnp.float32), "kv", split_axis=0, concat_axis=0, tiled=True
        ).astype(out_send.dtype),
        lax.all_to_all(top_send, "kv", split_axis=0, concat_axis=0, tiled=True),
        lax.all_to_all(total_send, "kv", split_axis=0, concat_axis=0, tiled=True),
    )
    top_entry = top_back.reshape((entries,) + top.shape[1:])
    total_entry = total_back.reshape((entries,) + total.shape[1:])
    out_entry = out_back.reshape((entries,) + out.shape[1:])
    grid = q_mine.reshape(steps, rows_group, kv_local, group, HD)
    fresh_keys = keys_mine.reshape(steps, rows_group, kv_local, HD)
    fresh_values = values_mine.reshape(steps, rows_group, kv_local, HD).astype(jnp.float32)
    new_scores = jnp.einsum(
        "tbkgc,ubkc->bktgu", grid, fresh_keys, preferred_element_type=jnp.float32
    ) * (1.0 / math.sqrt(HD))
    order = jnp.arange(steps, dtype=jnp.int32)
    causal = order[None, :] <= order[:, None]
    new_scores = jnp.where(causal[:, None, :], new_scores, -jnp.inf)
    new_top = jnp.max(new_scores, axis=-1)
    new_exp = jnp.exp(new_scores - new_top[..., None])
    new_total = jnp.sum(new_exp, axis=-1)
    new_out = jnp.einsum(
        "bktgu,ubkc->bktgc", new_exp, fresh_values, precision=lax.Precision.HIGHEST
    )
    member = entry_flat[None, :] == jnp.arange(rows_group, dtype=jnp.int32)[:, None]
    member_weight = member.astype(jnp.float32)
    entry_max = jnp.max(
        jnp.where(member[:, :, None, None, None], top_entry[None], -jnp.inf), axis=1
    )
    row_top = jnp.maximum(new_top, entry_max)
    top_at_entry = jnp.einsum(
        "be,bktg->ektg", member_weight, row_top, precision=lax.Precision.HIGHEST
    )
    entry_scale = jnp.where(
        entry_live[:, None, None, None], total_entry * jnp.exp(top_entry - top_at_entry), 0.0
    )
    new_scale = jnp.exp(new_top - row_top)
    row_total = new_total * new_scale + jnp.einsum(
        "be,ektg->bktg", member_weight, entry_scale, precision=lax.Precision.HIGHEST
    )
    weighted = entry_scale[..., None] * out_entry.astype(jnp.float32)
    numer = new_out * new_scale[..., None] + jnp.einsum(
        "be,ektgc->bktgc", member_weight, weighted, precision=lax.Precision.HIGHEST
    )
    result = numer / row_total[..., None]
    result = (
        jnp.transpose(result, (2, 0, 1, 3, 4))
        .reshape(steps, rows_group, width)
        .astype(jnp.bfloat16)
    )
    return lax.all_to_all(result, "tp", split_axis=1, concat_axis=2, tiled=True)


def solution(mesh):
    placed = (
        P(None, ("kv", "tp"), None),
        P(None, ("kv", "tp"), None),
        P(None, ("kv", "tp"), None),
        P("kv", None, "tp"),
        P("kv", None, "tp"),
        P(),
        P(),
    )
    return jax.shard_map(
        shards, mesh=mesh, in_specs=placed, out_specs=P(None, ("kv", "tp"), None), check_vma=False
    )
```

profile of v0, /device:TPU:8, one launch (start us, length us, event | category | flops | bytes accessed | tf_op | source)
XLA Modules:
  0.0 265.6 jit_solution(14856246588029737200)
XLA Ops:
  6.5 8.3 %copy.109 = bf16[3,2,8192]{0,1,2:T(2,128)(2,1)} copy(bf16[3,2,8192]{2,1,0:T(2,128)(2,1)} %param.7) | data formatting | bytes 196608 | tf_op args[0]
  14.9 6.8 %reshape.295 = bf16[4,2,6144]{2,1,0:T(2,128)(2,1)S(1)} reshape(bf16[8192,2,3]{2,1,0:T(2,128)(2,1)} %bitcast.104) | data formatting | bytes 196608
  21.7 9.9 %all_to_all.81 = bf16[4,2,6144]{2,1,0:T(2,128)(2,1)S(1)} all-to-all(bf16[4,2,6144]{2,1,0:T(2,128)(2,1)S(1)} %reshape.295), channel_id=1, replica_groups=mesh['kv'=64,'tp'=4] {'tp'}, dimensions={0} | all-to-all | bytes 196608 | tf_op jit(solution)/shard_map/all_to_all | solution.py:37
  31.6 9.8 %reshape.296 = bf16[8192,2,3]{2,1,0:T(2,128)(2,1)} reshape(bf16[4,2,6144]{2,1,0:T(2,128)(2,1)S(1)} %all_to_all.81) | data formatting | bytes 196608
  41.4 9.7 %copy.110 = bf16[3,2,4,2048]{3,1,2,0:T(2,128)(2,1)S(1)} copy(bf16[3,2,4,2048]{0,1,3,2:T(2,128)(2,1)} %bitcast.103) | data formatting | bytes 196608 | tf_op jit(solution)/shard_map/all_to_all | solution.py:37
  51.1 0.7 all_to_all.66
  51.8 0.5 copy.111
  52.3 1.3 reshape.301
  53.6 3.2 %all-to-all-start.1 = ((bf16[4,2,768]{2,1,0:T(2,128)(2,1)}), bf16[4,2,768]{2,1,0:T(2,128)(2,1)S(1)}, u32[]{:S(2)}, u32[]{:S(2)}) async-start(bf16[4,2,768]{2,1,0:T(2,128)(2,1)} %reshape.301), calls=%async_computation.1 | async-start | bytes 24576 | tf_op jit(solution)/shard_map/all_to_all | solution.py:38
  57.2 8.4 %reshape.276 = bf16[40,256,2,128]{3,2,1,0:T(2,128)(2,1)} reshape(bf16[40,256,256]{2,1,0:T(8,128)(2,1)} %param.10) | data formatting | bytes 10485760 | tf_op jit(solution)/shard_map/reshape | solution.py:15
  65.6 8.4 %reshape.278 = bf16[40,256,2,128]{3,2,1,0:T(2,128)(2,1)} reshape(bf16[40,256,256]{2,1,0:T(8,128)(2,1)} %param.11) | data formatting | bytes 10485760 | tf_op jit(solution)/shard_map/reshape | solution.py:16
  73.9 0.5 copy.115
  74.4 1.3 reshape.303
  75.8 2.0 select_reduce_fusion
  78.4 54.4 %all-gather.2.cloned.1.call-done = bf16[3,512,2048]{2,1,0:T(8,128)(2,1)} async-done(((bf16[3,8,2048]{2,1,0:T(8,128)(2,1)}), bf16[3,512,2048]{2,1,0:T(8,128)(2,1)}) %all-gather.2.cloned.1.call-update) | async-done | bytes 6291472 | tf_op jit(solution)/shard_map/all_gather | solution.py:86
  132.9 4.0 %convolution_convert_fusion = bf16[40,3,2048]{2,0,1:T(8,128)(2,1)S(1)} fusion(bf16[3,512,2048]{2,1,0:T(8,128)(2,1)} %all-gather.2.cloned.1.call-done, s32[40]{0:T(128)S(1)} %get-tuple-element.6), kind=kOutput, calls=%fused_computation.11 | convolution fusion | flops 251965440 | bytes 6783136 | tf_op jit(solution)/shard_map/sb,tbw->tsw/dot_general | solution.py:88
  137.0 4.2 %fusion.7 = (f32[40,2,3,8]{3,2,1,0:T(4,128)S(1)}, f32[40,2,3,8,256]{4,3,2,1,0:T(8,128)S(1)}) fusion(pred[40,256]{1,0:T(8,128)(4,1)S(1)} %iota_compare_fusion.4, bf16[40,256,2,128,1]{3,2,1,0,4:T(2,128)(2,1)} %bitcast.102, bf16[3,40,2,8,128]{4,3,2,1,0:T(8,128)(2,1)S(1)} %bitcast.116), kind=kOutput, calls=%fused_computation.15 | convolution fusion | flops 127301760 | bytes 7718400 | tf_op jit(solution)/shard_map/tskgc,snkc->sktgn/dot_general | solution.py:17
  141.3 1.0 fusion.9
  142.3 1.4 fusion.23
  143.8 4.3 %all-to-all-start.2 = ((bf16[4,2,768]{2,1,0:T(2,128)(2,1)}), bf16[4,2,768]{2,1,0:T(2,128)(2,1)S(1)}, u32[]{:S(2)}, u32[]{:S(2)}) async-start(bf16[4,2,768]{2,1,0:T(2,128)(2,1)} %reshape.303), calls=%async_computation.2 | async-start | bytes 24576 | tf_op jit(solution)/shard_map/all_to_all | solution.py:39
  148.4 0.4 copy.122
  148.7 1.2 reshape.299
  150.0 3.4 %all-to-all-done.2 = bf16[4,2,768]{2,1,0:T(2,128)(2,1)S(1)} async-done(((bf16[4,2,768]{2,1,0:T(2,128)(2,1)}), bf16[4,2,768]{2,1,0:T(2,128)(2,1)S(1)}, u32[]{:S(2)}, u32[]{:S(2)}) %all-to-all-start.2) | async-done | bytes 12320 | tf_op jit(solution)/shard_map/all_to_all | solution.py:39
  153.4 7.1 %all-to-all-start.3 = ((f32[64,1,144]{2,1,0:T(1,128)}), f32[64,1,144]{2,1,0:T(1,128)S(1)}, u32[]{:S(2)}, u32[]{:S(2)}) async-start(f32[64,1,144]{2,1,0:T(1,128)} %reshape.299), calls=%async_computation.3 | async-start | bytes 131072 | tf_op jit(solution)/shard_map/all_to_all | solution.py:108
  160.7 0.3 copy.127
  161.1 1.2 reshape.297
  162.3 7.0 %all-to-all-done.3 = f32[64,1,144]{2,1,0:T(1,128)S(1)} async-done(((f32[64,1,144]{2,1,0:T(1,128)}), f32[64,1,144]{2,1,0:T(1,128)S(1)}, u32[]{:S(2)}, u32[]{:S(2)}) %all-to-all-start.3) | async-done | bytes 36896 | tf_op jit(solution)/shard_map/all_to_all | solution.py:108
  169.3 5.5 %all-to-all-start.4 = ((f32[64,1,144]{2,1,0:T(1,128)}), f32[64,1,144]{2,1,0:T(1,128)S(1)}, u32[]{:S(2)}, u32[]{:S(2)}) async-start(f32[64,1,144]{2,1,0:T(1,128)} %reshape.297), calls=%async_computation.4 | async-start | bytes 131072 | tf_op jit(solution)/shard_map/all_to_all | solution.py:109
  174.8 0.9 convert_convert_fusion
  175.7 2.9 %copy.134 = bf16[192,2,3,8,128]{4,3,2,1,0:T(8,128)(2,1)} copy(bf16[192,2,3,8,128]{4,0,3,2,1:T(8,128)(2,1)S(1)} %convert_convert_fusion) | data formatting | bytes 4718592 | tf_op jit(solution)/shard_map/convert_element_type | solution.py:106
  178.7 5.0 %all-to-all-done.4 = f32[64,1,144]{2,1,0:T(1,128)S(1)} async-done(((f32[64,1,144]{2,1,0:T(1,128)}), f32[64,1,144]{2,1,0:T(1,128)S(1)}, u32[]{:S(2)}, u32[]{:S(2)}) %all-to-all-start.4) | async-done | bytes 36896 | tf_op jit(solution)/shard_map/all_to_all | solution.py:109
  183.7 5.6 %all-to-all-start.5 = ((bf16[64,3,2,3,8,128]{5,4,3,2,1,0:T(8,128)(2,1)}), bf16[64,3,2,3,8,128]{5,4,3,2,1,0:T(8,128)(2,1)S(1)}, u32[]{:S(2)}, u32[]{:S(2)}) async-start(bf16[64,3,2,3,8,128]{5,4,3,2,1,0:T(8,128)(2,1)} %bitcast.29), calls=%async_computation.5 | async-start | bytes 4718592 | tf_op jit(solution)/shard_map/all_to_all | solution.py:105
  189.3 0.4 convert_reduce_fusion
  190.1 1.0 reshape.302
  191.5 1.0 reshape.304
  193.0 0.4 fusion.78
  193.5 0.5 broadcast.356
  194.0 0.8 reduce.1
  194.8 0.4 reshape.300
  195.9 0.8 reduce
  196.7 0.4 reshape.298
  197.7 0.4 copy.131
  198.4 46.1 %all-to-all-done.5 = bf16[64,3,2,3,8,128]{5,4,3,2,1,0:T(8,128)(2,1)S(1)} async-done(((bf16[64,3,2,3,8,128]{5,4,3,2,1,0:T(8,128)(2,1)}), bf16[64,3,2,3,8,128]{5,4,3,2,1,0:T(8,128)(2,1)S(1)}, u32[]{:S(2)}, u32[]{:S(2)}) %all-to-all-start.5) | async-done | bytes 2359328 | tf_op jit(solution)/shard_map/all_to_all | solution.py:105
  244.5 1.4 convert_multiply_fusion
  246.0 2.9 %fusion.4 = f32[8,2,3,8,128]{4,0,3,2,1:T(8,128)S(1)} fusion(f32[192,2,3,8,128]{4,3,2,1,0:T(8,128)S(1)} %convert_multiply_fusion, s32[192]{0:T(256)S(1)} %select_reduce_fusion.1), kind=kOutput, calls=%fused_computation.6 | convolution fusion | flops 113247744 | bytes 4915968 | tf_op jit(solution)/shard_map/be,ektgc->bktgc/dot_general | solution.py:146
  248.8 0.4 fusion.13
  249.3 8.7 %all_to_all.82 = bf16[3,8,2048]{2,0,1:T(4,128)(2,1)S(1)} all-to-all(bf16[3,8,2048]{2,0,1:T(4,128)(2,1)S(1)} %reshape.294), channel_id=1, replica_groups=mesh['kv'=64,'tp'=4] {'tp'}, dimensions={1} | all-to-all | bytes 196608 | tf_op jit(solution)/shard_map/all_to_all | solution.py:155
  258.0 0.8 copy.159
  (58 shorter events, 4.5 us)
Async XLA Ops:
  6.5 126.3 %all-gather.2.cloned.1.call-start = ((), (), s32[]{:S(2)}) async-start(), calls=%async_computation.7 | async-start | bytes 6389760 | tf_op jit(solution)/shard_map/all_gather | solution.py:86
  31.6 20.2 %copy-start.1 = (bf16[3,2,1024]{2,1,0:T(2,128)(2,1)S(1)}, bf16[3,2,1024]{2,1,0:T(2,128)(2,1)}, u32[]{:S(2)}) copy-start(bf16[3,2,1024]{2,1,0:T(2,128)(2,1)} %param.8) | copy-start | bytes 36868
  31.6 25.3 %copy-start = (s32[512,128]{1,0:T(8,128)S(1)}, s32[512,128]{1,0:T(8,128)}, u32[]{:S(2)}) copy-start(s32[512,128]{1,0:T(8,128)} %param.13) | copy-start | bytes 786436
  53.6 90.1 %all-to-all-start.1 = ((bf16[4,2,768]{2,1,0:T(2,128)(2,1)}), bf16[4,2,768]{2,1,0:T(2,128)(2,1)S(1)}, u32[]{:S(2)}, u32[]{:S(2)}) async-start(bf16[4,2,768]{2,1,0:T(2,128)(2,1)} %reshape.301), calls=%async_computation.1 | async-start | bytes 24576 | tf_op jit(solution)/shard_map/all_to_all | solution.py:38
  65.6 8.4 %copy-start.2 = (bf16[3,2,1024]{2,1,0:T(2,128)(2,1)S(1)}, bf16[3,2,1024]{2,1,0:T(2,128)(2,1)}, u32[]{:S(2)}) copy-start(bf16[3,2,1024]{2,1,0:T(2,128)(2,1)} %param.9) | copy-start | bytes 36868
  65.6 12.2 %copy-start.3 = (s32[512]{0:T(512)S(1)}, s32[512]{0:T(512)}, u32[]{:S(2)}) copy-start(s32[512]{0:T(512)} %param.12) | copy-start | bytes 6148
  136.9 5.4 %slice-start = ((s8[5242880]{0:T(1024)(128)(4,1)}), s8[4194304]{0:T(1024)(128)(4,1)S(1)}, s32[]{:S(2)}) async-start(s8[5242880]{0:T(1024)(128)(4,1)} %bitcast.105), calls=%async_computation.8 | async-start | bytes 8388608
  137.0 5.3 %slice-start.1 = ((s8[5242880]{0:T(1024)(128)(4,1)}), s8[1048576]{0:T(1024)(128)(4,1)S(1)}, s32[]{:S(2)}) async-start(s8[5242880]{0:T(1024)(128)(4,1)} %bitcast.105), calls=%async_computation.9 | async-start | bytes 2097152
  143.8 9.6 %all-to-all-start.2 = ((bf16[4,2,768]{2,1,0:T(2,128)(2,1)}), bf16[4,2,768]{2,1,0:T(2,128)(2,1)S(1)}, u32[]{:S(2)}, u32[]{:S(2)}) async-start(bf16[4,2,768]{2,1,0:T(2,128)(2,1)} %reshape.303), calls=%async_computation.2 | async-start | bytes 24576 | tf_op jit(solution)/shard_map/all_to_all | solution.py:39
  153.4 15.9 %all-to-all-start.3 = ((f32[64,1,144]{2,1,0:T(1,128)}), f32[64,1,144]{2,1,0:T(1,128)S(1)}, u32[]{:S(2)}, u32[]{:S(2)}) async-start(f32[64,1,144]{2,1,0:T(1,128)} %reshape.299), calls=%async_computation.3 | async-start | bytes 131072 | tf_op jit(solution)/shard_map/all_to_all | solution.py:108
  169.3 14.4 %all-to-all-start.4 = ((f32[64,1,144]{2,1,0:T(1,128)}), f32[64,1,144]{2,1,0:T(1,128)S(1)}, u32[]{:S(2)}, u32[]{:S(2)}) async-start(f32[64,1,144]{2,1,0:T(1,128)} %reshape.297), calls=%async_computation.4 | async-start | bytes 131072 | tf_op jit(solution)/shard_map/all_to_all | solution.py:109
  183.7 60.9 %all-to-all-start.5 = ((bf16[64,3,2,3,8,128]{5,4,3,2,1,0:T(8,128)(2,1)}), bf16[64,3,2,3,8,128]{5,4,3,2,1,0:T(8,128)(2,1)S(1)}, u32[]{:S(2)}, u32[]{:S(2)}) async-start(bf16[64,3,2,3,8,128]{5,4,3,2,1,0:T(8,128)(2,1)} %bitcast.29), calls=%async_computation.5 | async-start | bytes 4718592 | tf_op jit(solution)/shard_map/all_to_all | solution.py:105
Sparse Core Ops, SparseCore 0:
  51.9 80.8 all-gather.1
where the time goes:
time: 268 us; the launch traced here: 266 us
  waiting for transfers between devices  116 us (43%)
  local copies, waits for them, and re-layouts  68.3 us (25%)
  starting transfers between devices  25.7 us (10%)
  blocking collectives  18.6 us (7%)
  matrix products  15.5 us (6%)
  between operations  13.8 us (5%)
  other arithmetic  7.69 us (3%)
    all_gather x1, waiting for transfers between devices, shards(): everyone = lax.all_gather(q_mine, 'kv', axis=1, tiled=True)  54.4 us
    all_to_all x1, waiting for transfers between devices, shards(): lax.all_to_all(out_send.astype(jnp.float32), 'kv', split_axis=0, concat_a...  46.1 us
    unnamed x26, local copies, waits for them, and re-layouts  34 us
    all_to_all x2, local copies, waits for them, and re-layouts, shards(): lax.all_to_all(queries, 'tp', split_axis=2, concat_axis=1, tiled=True)  10.4 us
    all_to_all x1, blocking collectives, shards(): lax.all_to_all(queries, 'tp', split_axis=2, concat_axis=1, tiled=True)  9.89 us
    all_to_all x1, blocking collectives, shards(): return lax.all_to_all(result, 'tp', split_axis=1, concat_axis=2, tiled=True)  8.72 us
    reshape x1, local copies, waits for them, and re-layouts, slot_partials(): values = value_cache.reshape(slots, value_cache.shape[1], kv_local, HD)  8.36 us
    reshape x1, local copies, waits for them, and re-layouts, slot_partials(): keys = key_cache.reshape(slots, key_cache.shape[1], kv_local, HD)  8.36 us
  transfers between devices with their start and end apart: 6, of which 5 were waited for; matrix products, arithmetic and copies ran while one was open for 19% of the time, Pallas kernels for 0%

commit v1 on v0

v1 whole, which is shorter than its diff:
```python
import functools
import heapq
import math

import jax
import jax.numpy as jnp
from jax import lax
from jax.experimental import pallas as pl
from jax.experimental.pallas import tpu as pltpu
from jax.sharding import PartitionSpec as P

HD = 128
NEG = -1e30
MESH = pl.DeviceIdType.MESH
F32 = jnp.float32
BF16 = jnp.bfloat16


class Dims:
    def __init__(self, ny, nz, ntp, rows_dev, slots, slot_len, steps, kv_local, group):
        self.ny, self.nz, self.ntp, self.rd = ny, nz, ntp, rows_dev
        self.slots, self.slot_len = slots, slot_len
        self.steps, self.kvl, self.group = steps, kv_local, group
        self.rg = rows_dev * ntp
        self.kv = ny * nz * 2
        self.rows = self.kv * self.rg
        self.q = steps * kv_local * group
        self.split = (5 * self.rg) // 8
        self.size = {"y": ny, "z": nz}
        self.hops = {a: (n // 2, n - 1 - n // 2) for a, n in self.size.items()}
        self.rows_of = ((0, self.split), (self.split, self.rg - self.split))


def gather_order(d):
    sizes = [n * d.q * HD * 2 for _, n in d.rows_of]
    free = {"y": 0.0, "z": 0.0}
    heap, order, count = [], [], [0]

    def send(now, msg):
        part, phase = msg[0], msg[1]
        axis = "zy"[part] if phase == 1 else "yz"[part]
        begin = max(now, free[axis])
        free[axis] = begin + sizes[part] / 100e3
        count[0] += 1
        heapq.heappush(heap, (free[axis] + 2.0, count[0], msg))

    for msg in gather_children(d, None):
        send(0.0, msg)
    while heap:
        now, _, msg = heapq.heappop(heap)
        order.append(msg)
        for child in gather_children(d, msg):
            send(now, child)
    return order


def gather_children(d, msg):
    out = []
    if msg is None:
        for phase in (1, 2):
            for part in (0, 1):
                axis = "zy"[part] if phase == 1 else "yz"[part]
                for way in (0, 1):
                    if d.hops[axis][way] >= 1:
                        out.append((part, phase, way, 1, 0))
        return out
    part, phase, way, j, oa = msg
    first, second = ("z", "y") if part == 0 else ("y", "z")
    axis = first if phase == 1 else second
    if j < d.hops[axis][way]:
        out.append((part, phase, way, j + 1, oa))
    if phase == 1:
        here = -j if way == 0 else j
        for w2 in (0, 1):
            if d.hops[second][w2] >= 1:
                out.append((part, 2, w2, 1, here))
    return out


def iota(shape, dim):
    return lax.broadcasted_iota(jnp.int32, shape, dim)


def slot_plan(d, kv, ps, ctx, out, pieces):
    partner = kv + 1 - 2 * lax.rem(kv, 2)
    core = lax.rem(kv, 2)
    chunks = d.rows // 128
    eye = iota((128, 128), 0) == iota((128, 128), 1)
    lane = iota((128, 128), 1)
    row_in = iota((128, 128), 0)

    def to_col(row):
        return jnp.sum(jnp.where(eye, jnp.broadcast_to(row, (128, 128)), 0), axis=1, keepdims=True)

    def to_row(col):
        return jnp.sum(jnp.where(eye, jnp.broadcast_to(col, (128, 128)), 0), axis=0, keepdims=True)

    zero = jnp.zeros((1, 128), jnp.int32)
    state = [[jnp.zeros((1, 1), jnp.int32), zero, zero] for _ in (0, 1)]

    def piece(side, c):
        base, acc_val, acc_row = state[side]
        owner = kv if side == 0 else partner
        local = ps[c * 128 : (c + 1) * 128, :] - owner * d.slots
        hit = (local >= 0) & (local < d.slots)
        many = jnp.sum(hit.astype(jnp.int32), axis=1, keepdims=True)
        many_row = to_row(many)
        before = jnp.sum(jnp.where(row_in < lane, many, 0), axis=0, keepdims=True)
        start_row = before + base
        last = jnp.where(many_row > 0, jnp.minimum(start_row + many_row - 1, d.slots), d.slots)
        out[5 + side * chunks + c : 6 + side * chunks + c, :] = last
        base = base + jnp.sum(many_row, axis=1, keepdims=True)
        start = to_col(start_row)
        if side == 0:
            length = to_col(ctx[c : c + 1, :])
            left = jnp.clip(length - lane * d.slot_len, 0, d.slot_len)
            far = 1 << 30
            code = jnp.where(hit, lane * 32768 + local * 512 + left, far)
        for k in range(3):
            at = (lane == start + k) & (many > k)
            acc_row += jnp.sum(jnp.where(at, row_in + c * 128, 0), axis=0, keepdims=True)
            if side == 0:
                first = jnp.min(code, axis=1, keepdims=True)
                code = jnp.where(code == first, far, code)
                acc_val += jnp.sum(jnp.where(at, lax.rem(first, 32768), 0), axis=0, keepdims=True)
        state[side] = [base, acc_val, acc_row]

    def finish():
        for side in (0, 1):
            _, acc_val, acc_row = state[side]
            mine = lax.rem(acc_row // d.rg, 2) == core
            place = (acc_row // (2 * d.rg)) * d.rg + lax.rem(acc_row, d.rg)
            place = jnp.clip(place, 0, d.rows // 2 - 1)
            if side == 0:
                same = (iota((1, 128), 1) > 0) & (pltpu.roll(acc_row, 1, 1) == acc_row)
                out[0:1, :] = jnp.where(mine, place, -1)
                out[1:2, :] = jnp.clip(acc_val // 512, 0, d.slots - 1)
                out[2:3, :] = lax.rem(acc_val, 512)
                out[3:4, :] = jnp.where(same, 1, 0)
            else:
                out[4:5, :] = jnp.where(mine, place, 0)

    for c in range(chunks):
        for side in (0, 1):
            pieces.append(functools.partial(piece, side, c))
    pieces.append(finish)


def main_kernel(
    d, order, ps, ctx, qx, nk, nv, kc, vc, out,
    psv, planv, meta, g, qp, qs, kb, vb, o, t, r0, r0s, r1, r1s, d0, d0s, d1, d1s, f, fs, rf, rfs,
    io_sem, kv_sem, tp_send, tp_recv, ag_send, ag_recv, fw_send, fw_recv, ex_send, ex_recv,
    s0_send, s0_recv, s1_send, s1_recv, fin_send, fin_recv,
):
    kv = lax.axis_index("kv")
    tp = lax.axis_index("tp")
    core = lax.rem(kv, 2)
    sgn = 1 - 2 * core
    chip = kv // 2
    pos = {"y": chip // d.nz, "z": lax.rem(chip, d.nz)}

    near = {}

    def coord(axis, k):
        n = d.size[axis]
        if (axis, k) not in near:
            near[axis, k] = lax.rem(pos[axis] + sgn * k + n, n)
        return near[axis, k]

    def chip_at(oy, oz):
        return coord("y", oy) * d.nz + coord("z", oz)

    def kv_at(oy, oz):
        return chip_at(oy, oz) * 2 + core

    def neighbour(axis, step):
        return (kv_at(step, 0) if axis == "y" else kv_at(0, step), tp)

    partner = (kv + sgn, tp)

    def remote(src, dst, ss, rs, dev):
        return pltpu.make_async_remote_copy(
            src_ref=src, dst_ref=dst, send_sem=ss, recv_sem=rs, device_id=dev, device_id_type=MESH
        )

    chunks = d.rows // 128

    ps_copy = pltpu.make_async_copy(ps, psv, io_sem.at[0])
    ps_copy.start()
    parts_kv = kv_sem.shape[1]
    per = d.slots // parts_kv
    kv_copies = []
    for n in range(parts_kv):
        for which, (src, dst) in enumerate(((kc, kb), (vc, vb))):
            cp = pltpu.make_async_copy(
                src.at[pl.ds(n * per, per)], dst.at[pl.ds(n * per, per)], kv_sem.at[which, n]
            )
            cp.start()
            kv_copies.append(cp)

    friends = [partner]
    for axis in ("y", "z"):
        for way in (0, 1):
            if d.hops[axis][way]:
                friends.append(neighbour(axis, 1 - 2 * way))
    for k in range(1, d.ntp):
        friends.append((kv, lax.rem(tp + k, d.ntp)))
    barrier = pltpu.get_barrier_semaphore()
    for dev in friends:
        pl.semaphore_signal(barrier, inc=1, device_id=dev, device_id_type=MESH)
    pl.semaphore_wait(barrier, len(friends))

    waits = []

    own = chip * d.rg
    tp_copies = []
    for k in range(1, d.ntp):
        other = lax.rem(tp + k, d.ntp)
        cp = remote(
            qx.at[other], g.at[pl.ds(own + tp * d.rd, d.rd)], tp_send.at[k - 1], tp_recv.at[k - 1], (kv, other)
        )
        cp.start()
        waits.append(cp)
    g[pl.ds(own + tp * d.rd, d.rd)] = qx[tp]
    for k in range(1, d.ntp):
        source = lax.rem(tp - k + d.ntp, d.ntp)
        remote(
            qx.at[tp], g.at[pl.ds(own + source * d.rd, d.rd)], tp_send.at[k - 1], tp_recv.at[k - 1], (kv, source)
        ).wait_recv()

    number = {msg: n for n, msg in enumerate(order)}

    def place(msg, back):
        part, phase, way, j, oa = msg
        turn = 1 if way == 0 else -1
        steps = j - 1 if back else j
        o1 = -turn * steps if phase == 1 else oa
        o2 = 0 if phase == 1 else -turn * steps
        oz, oy = (o1, o2) if part == 0 else (o2, o1)
        start, count = d.rows_of[part]
        return g.at[pl.ds(chip_at(oy, oz) * d.rg + start, count)]

    def ship(msg):
        part, phase, way, j, oa = msg
        axis = "zy"[part] if phase == 1 else "yz"[part]
        n = number[msg]
        src = place(msg, True)
        cp = remote(src, src, ag_send.at[n], ag_recv.at[n], neighbour(axis, 1 - 2 * way))
        cp.start()
        waits.append(cp)

    for msg in gather_children(d, None):
        ship(msg)
    ps_copy.wait()
    pieces = []
    slot_plan(d, kv, psv, ctx, planv, pieces)
    plan_copy = pltpu.make_async_copy(planv, meta, io_sem.at[1])
    for place_in, msg in enumerate(order):
        n = number[msg]
        landed = place(msg, False)
        remote(landed, landed, ag_send.at[n], ag_recv.at[n], partner).wait_recv()
        for child in gather_children(d, msg):
            ship(child)
        if place_in >= 8 and place_in % 3 == 0 and pieces:
            pieces.pop(0)()
    while pieces:
        pieces.pop(0)()
    plan_copy.start()
    plan_copy.wait()

    def pick(i, c):
        for u in range(4):
            qs[4 * i + u] = g[meta[4, 4 * i + u]]
        return c

    lax.fori_loop(0, d.slots // 4, pick, 0)
    cp = remote(qs, qp, fw_send.at[0], fw_recv.at[0], partner)
    cp.start()
    for copy in kv_copies:
        copy.wait()
    cp.wait()

    head = lax.rem(iota((d.q, 128), 0) // d.group, d.kvl)
    head_masks = [(head == k).astype(F32).astype(BF16) for k in range(d.kvl)]
    lane128 = iota((d.q, 128), 1)
    lane_slot = iota((d.q, d.slot_len), 1)
    scale = 1.0 / math.sqrt(HD)

    unroll = 4

    def attend_many(it, carry):
        m_p, l_p, o_p, mc, lc = carry
        at = [it * unroll + u for u in range(unroll)]
        rows = [meta[0, i] for i in at]
        qs = [jnp.where(row >= 0, g[jnp.maximum(row, 0)], qp[i]) for row, i in zip(rows, at)]
        q2 = [jnp.concatenate([q * mask for mask in head_masks], axis=1) for q in qs]
        slots = [meta[1, i] for i in at]
        score = [
            lax.dot_general(q, kb[slot], (((1,), (1,)), ((), ())), preferred_element_type=F32)
            for q, slot in zip(q2, slots)
        ]
        score = [jnp.where(lane_slot < meta[2, i], x * scale, NEG) for x, i in zip(score, at)]
        tops = [jnp.max(x, axis=1, keepdims=True) for x in score]
        ps = [jnp.exp(x - m) for x, m in zip(score, tops)]
        sums = [jnp.dot(p.astype(BF16), vb[slot], preferred_element_type=F32) for p, slot in zip(ps, slots)]
        totals = [jnp.sum(p, axis=1, keepdims=True) for p in ps]
        accs = []
        for u, i in enumerate(at):
            o_s = sums[u][:, :HD]
            for k in range(1, d.kvl):
                o_s = jnp.where(head == k, sums[u][:, k * HD : (k + 1) * HD], o_s)
            m_q = jnp.where(meta[3, i] > 0, m_p, NEG)
            m = jnp.maximum(m_q, tops[u])
            a, b = jnp.exp(m_q - m), jnp.exp(tops[u] - m)
            l_p = l_p * a + totals[u] * b
            o_p = o_p * a + o_s * b
            m_p = m
            accs.append(o_p.astype(BF16))
            mc = jnp.where(lane128 == i, m_p, mc)
            lc = jnp.where(lane128 == i, l_p, lc)
        for u, i in enumerate(at):
            o[0, i] = accs[u]
        return m_p, l_p, o_p, mc, lc

    zero_col = jnp.zeros((d.q, 1), F32)
    zero = jnp.zeros((d.q, 128), F32)
    _, _, _, mc, lc = lax.fori_loop(
        0, d.slots // unroll, attend_many, (zero_col, zero_col, zero, jnp.full((d.q, 128), NEG, F32), zero)
    )
    pad = jnp.zeros((128 - d.q, 128), F32)
    mt = jnp.transpose(jnp.concatenate([mc, pad], axis=0))
    lt = jnp.transpose(jnp.concatenate([lc, pad], axis=0))
    table = jnp.where(iota((128, 128), 1) < 64, mt, pltpu.roll(lt, 64, 1))
    spare = t.shape[1] - d.slots
    t[0] = table[: t.shape[1]]
    nobody = jnp.where(iota((spare, 128), 1) < 64, NEG, 0.0)
    for side in (0, 1):
        t[side, pl.ds(d.slots, spare)] = nobody
        o[side, d.slots] = jnp.zeros((d.q, 128), BF16)

    for n, ref in enumerate((o, t)):
        cp = remote(
            ref.at[0, pl.ds(0, d.slots)], ref.at[1, pl.ds(0, d.slots)], ex_send.at[n], ex_recv.at[n], partner
        )
        cp.start()
        waits.append(cp)
    for n, ref in enumerate((o, t)):
        remote(
            ref.at[0, pl.ds(0, d.slots)], ref.at[1, pl.ds(0, d.slots)], ex_send.at[n], ex_recv.at[n], partner
        ).wait_recv()

    lane8 = iota((8, 128), 1)

    def pad8(x):
        if x.shape[0] == 8:
            return x
        return jnp.concatenate([x, jnp.zeros((8 - x.shape[0], 128), F32)], axis=0)

    def prepare(stats, count):
        top = functools.reduce(jnp.maximum, stats)
        es = [jnp.exp(st - top) for st in stats]
        total = sum(e * pltpu.roll(st, 64, 1) for e, st in zip(es, stats))
        tile = jnp.where(lane8 < 64, top, pltpu.roll(total, 64, 1))[:count]
        return tile, jnp.transpose(jnp.concatenate(es, axis=0))

    def apply(tile, cols, rows, many, count, out_d, out_s):
        out_s[...] = tile
        for r in range(count):
            acc = None
            for k in range(many):
                term = rows(k, r).astype(F32) * cols[: d.q, k * 8 + r : k * 8 + r + 1]
                acc = term if acc is None else acc + term
            out_d[r] = acc.astype(BF16)

    def merge(jobs, count):
        tiles = [[pad8(x[1][...]) for x in ins] for ins, _ in jobs]
        ready = [prepare(stats, count) for stats in tiles]
        for (ins, dst), (tile, cols) in zip(jobs, ready):
            apply(tile, cols, lambda k, r: ins[k][0][r], len(ins), count, *dst)

    per_row = 128 // d.rg

    class Part:
        def __init__(self, first, second, rows, recv, recv_s, mine, mine_s, send_sem, recv_sem):
            self.first, self.second = first, second
            self.start, self.count = rows
            self.recv, self.recv_s, self.mine, self.mine_s = recv, recv_s, mine, mine_s
            self.send_sem, self.recv_sem = send_sem, recv_sem
            self.n1, self.lanes = d.size[first], d.size[second]
            self.h1, self.h2 = d.hops[first], d.hops[second]
            self.phase2 = sum(self.h1) * self.lanes
            self.to = {
                (axis, way): neighbour(axis, 1 - 2 * way) for axis in (first, second) for way in (0, 1)
            }

        def id1(self, way, j, lane):
            return (way * self.h1[0] + j - 1) * self.lanes + lane

        def id2(self, way, j):
            return self.phase2 + way * self.h2[0] + j - 1

        def bufs(self, n):
            return self.recv.at[n], self.recv_s.at[n]

        def chip_sum(self, o1, lane):
            n = (o1 % self.n1) * self.lanes + lane
            return self.mine.at[n], self.mine_s.at[n]

        def copies(self, src, n, axis, way):
            return [
                remote(a, b, self.send_sem.at[k, n], self.recv_sem.at[k, n], self.to[axis, way])
                for k, (a, b) in enumerate(zip(src, self.bufs(n)))
            ]

        def send(self, src, n, axis, way):
            for cp in self.copies(src, n, axis, way):
                cp.start()

        def wait(self, n):
            for cp in self.copies(self.bufs(n), n, self.first, 0):
                cp.wait_recv()

        def wait_sent(self, n):
            for cp in self.copies(self.bufs(n), n, self.first, 0):
                cp.wait_send()

        def lane(self, k):
            return (self.h2[0] + ((k + 1) // 2) * (1 if k % 2 else -1)) % self.lanes

        def build(self, offsets, k):
            lane = self.lane(k)
            jobs = []
            for o1 in offsets:
                oy, oz = (o1, lane) if self.first == "y" else (lane, o1)
                kv_to = kv_at(oy, oz)
                line, col = lax.div(kv_to, per_row), lax.rem(kv_to, per_row) * d.rg + self.start
                ids, stats = [], []
                for side in (0, 1):
                    ids.append([meta[5 + side * chunks + line, col + r] for r in range(self.count)])
                    stats.append(
                        pad8(jnp.concatenate([t[side, pl.ds(i, 1), :] for i in ids[side]], axis=0))
                    )
                jobs.append((ids, stats, self.chip_sum(o1, lane)))
            ready = [prepare(stats, self.count) for _, stats, _ in jobs]
            for (ids, _, dst), (tile, cols) in zip(jobs, ready):
                apply(tile, cols, lambda k, r: o[k, ids[k][r]], 2, self.count, *dst)

        def launch(self, k):
            ways = [way for way in (0, 1) if self.h1[way]]
            far = [(1 - 2 * way) * self.h1[way] for way in ways]
            self.build(far, k)
            lane = self.lane(k)
            for way, o1 in zip(ways, far):
                self.send(self.chip_sum(o1, lane), self.id1(way, 1, lane), self.first, way)

        def rest(self, k):
            for j in range(1, self.h1[0]):
                ways = [way for way in (0, 1) if j < self.h1[way]]
                self.build([(1 - 2 * way) * (self.h1[way] - j) for way in ways], k)
            self.build([0], k)

        def relay(self, j, k):
            lane = self.lane(k)
            ways = [way for way in (0, 1) if j < self.h1[way]]
            jobs = []
            for way in ways:
                n = self.id1(way, j, lane)
                self.wait(n)
                left = (1 - 2 * way) * (self.h1[way] - j)
                jobs.append(([self.bufs(n), self.chip_sum(left, lane)], self.bufs(n)))
            merge(jobs, self.count)
            for way, (_, src) in zip(ways, jobs):
                self.send(src, self.id1(way, j + 1, lane), self.first, way)

        def second_step(self, k, result):
            lane = self.lane(k)
            ids = [self.id1(way, self.h1[way], lane) for way in (0, 1) if self.h1[way]]
            last = k == self.lanes - 1
            if last:
                ids += [self.id2(way, self.h2[way]) for way in (0, 1) if self.h2[way]]
            elif k >= 2:
                ids.append(self.id2(k % 2, k // 2))
            for n in ids:
                self.wait(n)
            ins = [self.bufs(n) for n in ids] + [self.chip_sum(0, lane)]
            dst = result if last else ins[0]
            merge([(ins, dst)], self.count)
            if not last:
                self.send(dst, self.id2(k % 2, k // 2 + 1), self.second, k % 2)

        def drain(self):
            def body(n, c):
                self.wait_sent(n)
                return c

            lax.fori_loop(0, self.phase2 + sum(self.h2), body, 0)

    p0 = Part("y", "z", d.rows_of[0], r0, r0s, d0, d0s, s0_send, s0_recv)
    p1 = Part("z", "y", d.rows_of[1], r1, r1s, d1, d1s, s1_send, s1_recv)
    fin0 = (f.at[pl.ds(p0.start, p0.count)], fs.at[pl.ds(p0.start, p0.count)])
    fin1 = (f.at[pl.ds(p1.start, p1.count)], fs.at[pl.ds(p1.start, p1.count)])

    lag = 2
    steps = []
    for n, (p, fin) in enumerate(((p1, fin1), (p0, fin0))):
        last = p.lanes - 1
        for k in range(p.lanes):
            steps.append((k, 4, n, functools.partial(p.launch, k)))
            steps.append((k, 5, n, functools.partial(p.rest, k)))
            for j in range(1, p.h1[0]):
                steps.append((k + lag * j, 1, n, functools.partial(p.relay, j, k)))
            late = lag * p.h1[0] + k + (lag - 1 if k == last else 0)
            steps.append((late, 3, n, functools.partial(p.second_step, k, fin)))
    steps.sort(key=lambda x: x[:3])
    for _, _, _, run in steps:
        run()

    for n in range(d.ntp):
        for i in range(d.rd):
            rfs_row = fs[n * d.rd + i : n * d.rd + i + 1, :]
            b1s_tmp = rfs_row
            rfs.at[d.ntp + n][i : i + 1, :] = b1s_tmp

    def final(k, dst_t, src_t, dev_t):
        return [
            remote(f.at[pl.ds(src_t * d.rd, d.rd)], rf.at[dst_t], fin_send.at[0, k], fin_recv.at[0, k], (kv, dev_t)),
            remote(rfs.at[d.ntp + src_t], rfs.at[dst_t], fin_send.at[1, k], fin_recv.at[1, k], (kv, dev_t)),
        ]

    for k in range(1, d.ntp):
        other = lax.rem(tp + k, d.ntp)
        for cp in final(k - 1, tp, other, other):
            cp.start()
            waits.append(cp)
    rf[tp] = f[pl.ds(tp * d.rd, d.rd)]
    rfs[tp] = rfs[d.ntp + tp]

    nkf, nvf = nk[...].astype(F32), nv[...].astype(F32)
    fresh = []
    for h in range(d.ntp):
        for i in range(d.rd):
            tops, totals, outs = [], [], []
            qf = qx[h, i].astype(F32)
            for step in range(d.steps):
                for k in range(d.kvl):
                    at = (step * d.kvl + k) * d.group
                    kk = h * d.kvl + k
                    qs = qf[at : at + d.group]
                    scores = [
                        jnp.sum(qs * nkf[u, i, kk : kk + 1, :], axis=1, keepdims=True) * scale
                        for u in range(step + 1)
                    ]
                    top = functools.reduce(jnp.maximum, scores)
                    ws = [jnp.exp(x - top) for x in scores]
                    tops.append(top)
                    totals.append(sum(ws))
                    outs.append(sum(w * nvf[u, i, kk : kk + 1, :] for u, w in enumerate(ws)))
            fresh.append([jnp.concatenate(x, axis=0) for x in (tops, totals, outs)])

    for k in range(1, d.ntp):
        source = lax.rem(tp - k + d.ntp, d.ntp)
        for cp in final(k - 1, source, tp, source):
            cp.wait_recv()
    for h in range(d.ntp):
        cols = jnp.transpose(pad8(rfs[h]))
        for i in range(d.rd):
            top_n, total_n, out_n = fresh[h * d.rd + i]
            top_c, total_c = cols[: d.q, i : i + 1], cols[64 : 64 + d.q, i : i + 1]
            top = jnp.maximum(top_n, top_c)
            a, b = jnp.exp(top_n - top), jnp.exp(top_c - top)
            numer = out_n * a + rf[h, i].astype(F32) * b
            out[h, i] = (numer / (total_n * a + total_c * b)).astype(BF16)

    for cp in waits:
        cp.wait_send()
    p0.drain()
    p1.drain()


def make_shards(d):
    order = gather_order(d)

    def shards(queries, new_keys, new_values, key_cache, value_cache, context_lengths, piece_slots):
        steps, rd, width = queries.shape
        chunks = d.rows // 128
        vmem = pl.BlockSpec(memory_space=pltpu.VMEM)
        hbm = pl.BlockSpec(memory_space=pl.ANY)
        qh = queries.reshape(steps, rd, d.ntp, d.kvl * d.group, HD)
        qx = jnp.transpose(qh, (2, 1, 0, 3, 4)).reshape(d.ntp, rd, d.q, HD)
        nk = new_keys.reshape(steps, rd, d.ntp * d.kvl, HD)
        nv = new_values.reshape(steps, rd, d.ntp * d.kvl, HD)
        c0, c1 = d.rows_of[0][1], d.rows_of[1][1]
        n0 = sum(d.hops["y"]) * d.nz + sum(d.hops["z"])
        n1 = sum(d.hops["z"]) * d.ny + sum(d.hops["y"])
        pad = d.slots + 8
        dma = pltpu.SemaphoreType.DMA
        sem = lambda *shape: dma(shape)
        nt = max(d.ntp - 1, 1)
        plan_rows = -(-(5 + 2 * chunks) // 8) * 8
        scratch = [
            pltpu.VMEM(piece_slots.shape, jnp.int32),
            pltpu.VMEM((plan_rows, 128), jnp.int32),
            pltpu.SMEM((plan_rows, 128), jnp.int32),
            pltpu.VMEM((d.rows // 2, d.q, HD), BF16),
            pltpu.VMEM((d.slots, d.q, HD), BF16),
            pltpu.VMEM((d.slots, d.q, HD), BF16),
            pltpu.VMEM(key_cache.shape, BF16),
            pltpu.VMEM(value_cache.shape, BF16),
            pltpu.VMEM((2, pad, d.q, HD), BF16),
            pltpu.VMEM((2, pad, 128), F32),
            pltpu.VMEM((n0, c0, d.q, HD), BF16),
            pltpu.VMEM((n0, c0, 128), F32),
            pltpu.VMEM((n1, c1, d.q, HD), BF16),
            pltpu.VMEM((n1, c1, 128), F32),
            pltpu.VMEM((d.ny * d.nz, c0, d.q, HD), BF16),
            pltpu.VMEM((d.ny * d.nz, c0, 128), F32),
            pltpu.VMEM((d.ny * d.nz, c1, d.q, HD), BF16),
            pltpu.VMEM((d.ny * d.nz, c1, 128), F32),
            pltpu.VMEM((d.rg, d.q, HD), BF16),
            pltpu.VMEM((d.rg, 128), F32),
            pltpu.VMEM((d.ntp, rd, d.q, HD), BF16),
            pltpu.VMEM((2 * d.ntp, rd, 128), F32),
            sem(2), sem(2, 4), sem(nt), sem(nt), sem(len(order)), sem(len(order)), sem(1), sem(1),
            sem(2), sem(2), sem(2, n0), sem(2, n0), sem(2, n1), sem(2, n1), sem(2, nt), sem(2, nt),
        ]
        result = pl.pallas_call(
            functools.partial(main_kernel, d, order),
            out_shape=jax.ShapeDtypeStruct((d.ntp, rd, d.q, HD), BF16),
            in_specs=[hbm, vmem, vmem, vmem, vmem, hbm, hbm],
            out_specs=vmem,
            scratch_shapes=scratch,
            compiler_params=pltpu.CompilerParams(
                collective_id=0, has_side_effects=True, vmem_limit_bytes=60 * 1024 * 1024
            ),
        )(piece_slots, context_lengths.reshape(chunks, 128), qx, nk, nv, key_cache, value_cache)
        result = result.reshape(d.ntp, rd, steps, d.kvl * d.group, HD)
        return jnp.transpose(result, (2, 1, 0, 3, 4)).reshape(steps, rd, width)

    return shards


def solution(mesh):
    d = Dims(4, 8, 4, 2, 40, 256, 3, 2, 8)
    return build(mesh, d)


def build(mesh, d):
    placed = (
        P(None, ("kv", "tp"), None),
        P(None, ("kv", "tp"), None),
        P(None, ("kv", "tp"), None),
        P("kv", None, "tp"),
        P("kv", None, "tp"),
        P(),
        P(),
    )
    return jax.shard_map(
        make_shards(d),
        mesh=mesh,
        in_specs=placed,
        out_specs=P(None, ("kv", "tp"), None),
        check_vma=False,
    )
```

time: 268 us -> 90.4 us (0.34)
  waiting for transfers between devices: 116 us -> 0 us
  Pallas kernels: 0 us -> 84.3 us
  local copies, waits for them, and re-layouts: 68.3 us -> 5.83 us
  starting transfers between devices: 25.7 us -> 0 us
  blocking collectives: 18.6 us -> 0 us
  matrix products: 15.5 us -> 0 us
  between operations: 13.8 us -> 0.01 us
  other arithmetic: 7.69 us -> 0 us
    pallas_call x0 -> x1, Pallas kernels: none -> 84.3 us  [shards(): pl.pallas_call(functools.partial(main_kernel, d, order), out_shape=jax.Sh...]
    all_to_all x5 -> x0, waiting for transfers between devices: 61.5 us -> none  [the longest x1 46.1 us: shards(): lax.all_to_all(out_send.astype(jnp.float32), 'kv', split_axis=0, concat_a...]
    all_gather x1 -> x0, waiting for transfers between devices: 54.4 us -> none  [shards(): everyone = lax.all_gather(q_mine, 'kv', axis=1, tiled=True)]
    unnamed x26 -> x0, local copies, waits for them, and re-layouts: 34 us -> none
    all_to_all x5 -> x0, starting transfers between devices: 25.7 us -> none  [the longest x1 7.11 us: shards(): lax.all_to_all(top_send, 'kv', split_axis=0, concat_axis=0, tiled=True)]
    all_to_all x2 -> x0, blocking collectives: 18.6 us -> none  [the longest x1 9.89 us: shards(): lax.all_to_all(queries, 'tp', split_axis=2, concat_axis=1, tiled=True)]
    dot_general x11 -> x0, matrix products: 15.3 us -> none  [the longest x1 4.24 us: slot_partials(): jnp.einsum('tskgc,snkc->sktgn', grid, keys, preferred_element_type=jnp.fl...]
    reshape x7 -> x5, local copies, waits for them, and re-layouts: 17.3 us -> 4.93 us  [the longest x2 1.62 us: shards(): qh = queries.reshape(steps, rd, d.ntp, d.kvl * d.group, HD)]
  transfers between devices with their start and end apart: 6 -> 0, of which waited for: 5 -> 0; matrix products, arithmetic and copies ran while one was open for 19% -> 0% of each run, Pallas kernels for 0% -> 0%
where the time goes in v1:
time: 90.4 us; the launch traced here: 90.1 us
  Pallas kernels  84.3 us (93%)
  local copies, waits for them, and re-layouts  5.83 us (6%)
    pallas_call x1, Pallas kernels, shards(): pl.pallas_call(functools.partial(main_kernel, d, order), out_shape=jax.Sh...  84.3 us

profile of v1, /device:TPU:8, one launch (start us, length us, event | category | flops | bytes accessed | tf_op | source)
XLA Modules:
  0.0 90.1 jit_solution(7818409680266124430)
XLA Ops:
  0.0 1.3 %reshape.24.nk = bf16[3,2,8,128]{3,2,1,0:T(8,128)(2,1)} reshape(bf16[3,2,1024]{2,1,0:T(2,128)(2,1)} %param.8) | data formatting | bytes 24576 | tf_op jit(solution)/shard_map/reshape | solution.py:590
  1.3 1.3 %reshape.25.nv = bf16[3,2,8,128]{3,2,1,0:T(8,128)(2,1)} reshape(bf16[3,2,1024]{2,1,0:T(2,128)(2,1)} %param.9) | data formatting | bytes 24576 | tf_op jit(solution)/shard_map/reshape | solution.py:591
  2.6 1.0 %reshape.22 = bf16[3,2,4,16,128]{4,3,2,1,0:T(8,128)(2,1)S(1)} reshape(bf16[3,2,8192]{2,1,0:T(2,128)(2,1)} %param.7) | data formatting | bytes 196608 | tf_op jit(solution)/shard_map/reshape | solution.py:588
  3.6 0.6 copy.8
  4.3 84.3 %shard_map.73 = bf16[4,2,48,128]{3,2,1,0:T(8,128)(2,1)} custom-call(s32[512,128]{1,0:T(8,128)} %ps.1, s32[4,128]{1,0:T(4,128)} %bitcast.11, bf16[4,2,48,128]{3,2,1,0:T(8,128)(2,1)} %bitcast.9, bf16[3,2,8,128]{3,2,1,0:T(8,128)(2,1)} %reshape.24.nk, bf16[3,2,8,128]{3,2,1,0:T(8,128)(2,1)} %reshape.25.nv, bf16[40,256,256]{2,1,0:T(8,128)(2,1)} %kc.1, ...), custom_call_target="tpu_custom_call" | custom-call | tf_op jit(solution)/shard_map/pallas_call | solution.py:626
  88.6 0.9 copy.9
  89.5 0.7 reshape.27

commit v2 on v1

--- a/solution.py
+++ b/solution.py
@@ -1,5 +1,4 @@
 import functools
-import heapq
 import math
 
 import jax
@@ -31,27 +30,60 @@
         self.rows_of = ((0, self.split), (self.split, self.rg - self.split))
 
 
-def gather_order(d):
-    sizes = [n * d.q * HD * 2 for _, n in d.rows_of]
-    free = {"y": 0.0, "z": 0.0}
-    heap, order, count = [], [], [0]
-
-    def send(now, msg):
-        part, phase = msg[0], msg[1]
-        axis = "zy"[part] if phase == 1 else "yz"[part]
-        begin = max(now, free[axis])
-        free[axis] = begin + sizes[part] / 100e3
-        count[0] += 1
-        heapq.heappush(heap, (free[axis] + 2.0, count[0], msg))
-
-    for msg in gather_children(d, None):
-        send(0.0, msg)
-    while heap:
-        now, _, msg = heapq.heappop(heap)
-        order.append(msg)
+def list_order(tasks, limit, latency=1.75, rate=95e3, tick=0.02):
+    left = {t[0]: t for t in tasks}
+    flying = {"y": [], "z": []}
+    arrived, order = {}, []
+    now, busy, running = 0.0, 0.0, None
+    while left or running:
+        if now >= busy - 1e-9:
+            if running:
+                for msg, axis, size in running[4]:
+                    flying[axis].append([msg, size])
+                running = None
+            ready, urgent = [], set()
+            for name, _, waits, before, _, paced, rank in left.values():
+                if any(arrived.get(w, 1e9) > now for w in waits):
+                    continue
+                if any(x in left for x in before):
+                    urgent.update(before)
+                elif not paced or len(flying[paced]) < limit:
+                    ready.append((rank, name))
+            ready = [((0.5,) + r[1:] if n in urgent and r[0] > 0.5 else r, n) for r, n in ready]
+            if ready:
+                name = min(ready)[1]
+                running = left.pop(name)
+                order.append(name)
+                busy = now + running[1]
+        for axis, copies in flying.items():
+            for c in copies:
+                c[1] -= rate * tick / len(copies)
+                if c[1] <= 0:
+                    arrived[c[0]] = now + tick + latency
+            flying[axis] = [c for c in copies if c[1] > 0]
+        now += tick
+    return order
+
+
+def gather_order(d, limit=2):
+    tasks, depth = [], {}
+
+    def hops(msg):
+        return max([1 + hops(c) for c in gather_children(d, msg)], default=0)
+
+    def add(msg):
         for child in gather_children(d, msg):
-            send(now, child)
-    return order
+            part, phase = child[0], child[1]
+            axis = "zy"[part] if phase == 1 else "yz"[part]
+            size = d.rows_of[part][1] * d.q * HD * 2
+            before = [("wait", msg)] if msg else []
+            rank = (0, -hops(child), len(tasks))
+            tasks.append((("send", child), 0.06, [], before, [(child, axis, size)], axis, rank))
+            tasks.append((("wait", child), 0.12, [child], [], [], None, (1, 0, len(tasks))))
+            add(child)
+
+    add(None)
+    return list_order(tasks, limit)
 
 
 def gather_children(d, msg):
@@ -147,8 +179,8 @@
 
 
 def main_kernel(
-    d, order, ps, ctx, qx, nk, nv, kc, vc, out,
-    psv, planv, meta, g, qp, qs, kb, vb, o, t, r0, r0s, r1, r1s, d0, d0s, d1, d1s, f, fs, rf, rfs,
+    d, order, ps, ctx, q_in, nk_in, nv_in, kc, vc, out,
+    q_raw, nk, nv, stage, wide, qx, psv, planv, meta, g, qp, qs, kb, vb, o, t, r0, r0s, r1, r1s, d0, d0s, d1, d1s, f, fs, rf, rfs,
     io_sem, kv_sem, tp_send, tp_recv, ag_send, ag_recv, fw_send, fw_recv, ex_send, ex_recv,
     s0_send, s0_recv, s1_send, s1_recv, fin_send, fin_recv,
 ):
@@ -185,6 +217,14 @@
 
     chunks = d.rows // 128
 
+    q_copy = pltpu.make_async_copy(q_in, q_raw, io_sem.at[2])
+    q_copy.start()
+    new_copies = [
+        pltpu.make_async_copy(src, dst, io_sem.at[n])
+        for n, (src, dst) in enumerate(((nk_in, nk), (nv_in, nv)), 3)
+    ]
+    for cp in new_copies:
+        cp.start()
     ps_copy = pltpu.make_async_copy(ps, psv, io_sem.at[0])
     ps_copy.start()
     parts_kv = kv_sem.shape[1]
@@ -208,6 +248,17 @@
     barrier = pltpu.get_barrier_semaphore()
     for dev in friends:
         pl.semaphore_signal(barrier, inc=1, device_id=dev, device_id_type=MESH)
+
+    q_copy.wait()
+    heads = d.kvl * d.group
+    for step in range(d.steps):
+        q_step = q_raw[step].astype(F32)
+        for h in range(d.ntp):
+            for i in range(d.rd):
+                for j in range(heads):
+                    at = (h * heads + j) * HD
+                    stage[h, i, pl.ds(step * heads + j, 1), :] = q_step[i : i + 1, at : at + HD]
+    qx[...] = stage[...].astype(BF16)
     pl.semaphore_wait(barrier, len(friends))
 
     waits = []
@@ -228,7 +279,7 @@
             qx.at[tp], g.at[pl.ds(own + source * d.rd, d.rd)], tp_send.at[k - 1], tp_recv.at[k - 1], (kv, source)
         ).wait_recv()
 
-    number = {msg: n for n, msg in enumerate(order)}
+    number = {msg: n for n, msg in enumerate(msg for what, msg in order if what == "send")}
 
     def place(msg, back):
         part, phase, way, j, oa = msg
@@ -249,19 +300,18 @@
         cp.start()
         waits.append(cp)
 
-    for msg in gather_children(d, None):
-        ship(msg)
     ps_copy.wait()
     pieces = []
     slot_plan(d, kv, psv, ctx, planv, pieces)
     plan_copy = pltpu.make_async_copy(planv, meta, io_sem.at[1])
-    for place_in, msg in enumerate(order):
+    for place_in, (what, msg) in enumerate(order):
+        if what == "send":
+            ship(msg)
+            continue
         n = number[msg]
         landed = place(msg, False)
         remote(landed, landed, ag_send.at[n], ag_recv.at[n], partner).wait_recv()
-        for child in gather_children(d, msg):
-            ship(child)
-        if place_in >= 8 and place_in % 3 == 0 and pieces:
+        if place_in >= 24 and place_in % 3 == 0 and pieces:
             pieces.pop(0)()
     while pieces:
         pieces.pop(0)()
@@ -535,7 +585,10 @@
     rf[tp] = f[pl.ds(tp * d.rd, d.rd)]
     rfs[tp] = rfs[d.ntp + tp]
 
-    nkf, nvf = nk[...].astype(F32), nv[...].astype(F32)
+    for cp in new_copies:
+        cp.wait()
+    nkf = [nk[u].astype(F32) for u in range(d.steps)]
+    nvf = [nv[u].astype(F32) for u in range(d.steps)]
     fresh = []
     for h in range(d.ntp):
         for i in range(d.rd):
@@ -547,14 +600,14 @@
                     kk = h * d.kvl + k
                     qs = qf[at : at + d.group]
                     scores = [
-                        jnp.sum(qs * nkf[u, i, kk : kk + 1, :], axis=1, keepdims=True) * scale
+                        jnp.sum(qs * nkf[u][i : i + 1, kk * HD : (kk + 1) * HD], axis=1, keepdims=True) * scale
                         for u in range(step + 1)
                     ]
                     top = functools.reduce(jnp.maximum, scores)
                     ws = [jnp.exp(x - top) for x in scores]
                     tops.append(top)
                     totals.append(sum(ws))
-                    outs.append(sum(w * nvf[u, i, kk : kk + 1, :] for u, w in enumerate(ws)))
+                    outs.append(sum(w * nvf[u][i : i + 1, kk * HD : (kk + 1) * HD] for u, w in enumerate(ws)))
             fresh.append([jnp.concatenate(x, axis=0) for x in (tops, totals, outs)])
 
     for k in range(1, d.ntp):
@@ -569,7 +622,14 @@
             top = jnp.maximum(top_n, top_c)
             a, b = jnp.exp(top_n - top), jnp.exp(top_c - top)
             numer = out_n * a + rf[h, i].astype(F32) * b
-            out[h, i] = (numer / (total_n * a + total_c * b)).astype(BF16)
+            stage[h, i] = numer / (total_n * a + total_c * b)
+    for step in range(d.steps):
+        for h in range(d.ntp):
+            for i in range(d.rd):
+                for j in range(heads):
+                    at = (h * heads + j) * HD
+                    wide[i : i + 1, at : at + HD] = stage[h, i, pl.ds(step * heads + j, 1), :]
+        out[step] = wide[...].astype(BF16)
 
     for cp in waits:
         cp.wait_send()
@@ -585,10 +645,6 @@
         chunks = d.rows // 128
         vmem = pl.BlockSpec(memory_space=pltpu.VMEM)
         hbm = pl.BlockSpec(memory_space=pl.ANY)
-        qh = queries.reshape(steps, rd, d.ntp, d.kvl * d.group, HD)
-        qx = jnp.transpose(qh, (2, 1, 0, 3, 4)).reshape(d.ntp, rd, d.q, HD)
-        nk = new_keys.reshape(steps, rd, d.ntp * d.kvl, HD)
-        nv = new_values.reshape(steps, rd, d.ntp * d.kvl, HD)
         c0, c1 = d.rows_of[0][1], d.rows_of[1][1]
         n0 = sum(d.hops["y"]) * d.nz + sum(d.hops["z"])
         n1 = sum(d.hops["z"]) * d.ny + sum(d.hops["y"])
@@ -598,6 +654,12 @@
         nt = max(d.ntp - 1, 1)
         plan_rows = -(-(5 + 2 * chunks) // 8) * 8
         scratch = [
+            pltpu.VMEM(queries.shape, BF16),
+            pltpu.VMEM(new_keys.shape, BF16),
+            pltpu.VMEM(new_values.shape, BF16),
+            pltpu.VMEM((d.ntp, rd, d.q, HD), F32),
+            pltpu.VMEM((rd, width), F32),
+            pltpu.VMEM((d.ntp, rd, d.q, HD), BF16),
             pltpu.VMEM(piece_slots.shape, jnp.int32),
             pltpu.VMEM((plan_rows, 128), jnp.int32),
             pltpu.SMEM((plan_rows, 128), jnp.int32),
@@ -620,21 +682,20 @@
             pltpu.VMEM((d.rg, 128), F32),
             pltpu.VMEM((d.ntp, rd, d.q, HD), BF16),
             pltpu.VMEM((2 * d.ntp, rd, 128), F32),
-            sem(2), sem(2, 4), sem(nt), sem(nt), sem(len(order)), sem(len(order)), sem(1), sem(1),
+            sem(5), sem(2, 4), sem(nt), sem(nt), sem(len(order) // 2), sem(len(order) // 2), sem(1), sem(1),
             sem(2), sem(2), sem(2, n0), sem(2, n0), sem(2, n1), sem(2, n1), sem(2, nt), sem(2, nt),
         ]
         result = pl.pallas_call(
             functools.partial(main_kernel, d, order),
-            out_shape=jax.ShapeDtypeStruct((d.ntp, rd, d.q, HD), BF16),
-            in_specs=[hbm, vmem, vmem, vmem, vmem, hbm, hbm],
+            out_shape=jax.ShapeDtypeStruct(queries.shape, BF16),
+            in_specs=[hbm, vmem, hbm, hbm, hbm, hbm, hbm],
             out_specs=vmem,
             scratch_shapes=scratch,
             compiler_params=pltpu.CompilerParams(
                 collective_id=0, has_side_effects=True, vmem_limit_bytes=60 * 1024 * 1024
             ),
-        )(piece_slots, context_lengths.reshape(chunks, 128), qx, nk, nv, key_cache, value_cache)
-        result = result.reshape(d.ntp, rd, steps, d.kvl * d.group, HD)
-        return jnp.transpose(result, (2, 1, 0, 3, 4)).reshape(steps, rd, width)
+        )(piece_slots, context_lengths.reshape(chunks, 128), queries, new_keys, new_values, key_cache, value_cache)
+        return result
 
     return shards
 

time: 90.4 us -> 87.5 us (0.968)
  local copies, waits for them, and re-layouts: 5.83 us -> 1.6 us
  Pallas kernels: 84.3 us -> 85.7 us
    reshape x5 -> x0, local copies, waits for them, and re-layouts: 4.93 us -> none  [the longest x2 1.62 us: shards(): qh = queries.reshape(steps, rd, d.ntp, d.kvl * d.group, HD)]
    unnamed x0 -> x1, local copies, waits for them, and re-layouts: none -> 1.6 us
    pallas_call x1, Pallas kernels: 84.3 us -> 85.7 us  [shards(): pl.pallas_call(functools.partial(main_kernel, d, order), out_shape=jax.Sh...]
where the time goes in v2:
time: 87.5 us; the launch traced here: 87.3 us
  Pallas kernels  85.7 us (98%)
  local copies, waits for them, and re-layouts  1.6 us (2%)
    pallas_call x1, Pallas kernels, shards(): pl.pallas_call(functools.partial(main_kernel, d, order), out_shape=jax.Sh...  85.7 us

profile of v2, /device:TPU:8, one launch (start us, length us, event | category | flops | bytes accessed | tf_op | source)
XLA Modules:
  0.0 87.3 jit_solution(7504088157372659789)
XLA Ops:
  0.0 85.7 %shard_map.73 = bf16[3,2,8192]{2,1,0:T(2,128)(2,1)} custom-call(s32[512,128]{1,0:T(8,128)} %ps.1, s32[4,128]{1,0:T(4,128)} %bitcast.1, bf16[3,2,8192]{2,1,0:T(2,128)(2,1)} %q_in.1, bf16[3,2,1024]{2,1,0:T(2,128)(2,1)} %nk_in.1, bf16[3,2,1024]{2,1,0:T(2,128)(2,1)} %nv_in.1, bf16[40,256,256]{2,1,0:T(8,128)(2,1)} %kc.1, bf16[40,256,256]{2,1,0:T(8,128)(2,1)} %vc.1), custom_call_target="tpu_custom_call" | custom-call | tf_op jit(solution)/shard_map/pallas_call | solution.py:688
  85.7 1.6 %copy.9 = bf16[3,2,8192]{2,1,0:T(2,128)(2,1)} copy(bf16[3,2,8192]{2,1,0:T(2,128)(2,1)} %shard_map.73) | data formatting | bytes 196608

commit v3 on v2

--- a/solution.py
+++ b/solution.py
@@ -180,7 +180,7 @@
 
 def main_kernel(
     d, order, ps, ctx, q_in, nk_in, nv_in, kc, vc, out,
-    q_raw, nk, nv, stage, wide, qx, psv, planv, meta, g, qp, qs, kb, vb, o, t, r0, r0s, r1, r1s, d0, d0s, d1, d1s, f, fs, rf, rfs,
+    q_raw, nk, nv, stage, qx, psv, planv, meta, g, qp, qs, kb, vb, o, t, r0, r0s, r1, r1s, d0, d0s, d1, d1s, f, fs, rf, rfs,
     io_sem, kv_sem, tp_send, tp_recv, ag_send, ag_recv, fw_send, fw_recv, ex_send, ex_recv,
     s0_send, s0_recv, s1_send, s1_recv, fin_send, fin_recv,
 ):
@@ -311,11 +311,14 @@
         n = number[msg]
         landed = place(msg, False)
         remote(landed, landed, ag_send.at[n], ag_recv.at[n], partner).wait_recv()
-        if place_in >= 24 and place_in % 3 == 0 and pieces:
+        if place_in >= 16 and pieces:
             pieces.pop(0)()
-    while pieces:
-        pieces.pop(0)()
-    plan_copy.start()
+            if not pieces:
+                plan_copy.start()
+    if pieces:
+        while pieces:
+            pieces.pop(0)()
+        plan_copy.start()
     plan_copy.wait()
 
     def pick(i, c):
@@ -326,8 +329,11 @@
     lax.fori_loop(0, d.slots // 4, pick, 0)
     cp = remote(qs, qp, fw_send.at[0], fw_recv.at[0], partner)
     cp.start()
-    for copy in kv_copies:
+    for copy in kv_copies + new_copies:
         copy.wait()
+    for other in waits:
+        other.wait_send()
+    waits.clear()
     cp.wait()
 
     head = lax.rem(iota((d.q, 128), 0) // d.group, d.kvl)
@@ -336,7 +342,7 @@
     lane_slot = iota((d.q, d.slot_len), 1)
     scale = 1.0 / math.sqrt(HD)
 
-    unroll = 4
+    unroll = 8
 
     def attend_many(it, carry):
         m_p, l_p, o_p, mc, lc = carry
@@ -585,8 +591,6 @@
     rf[tp] = f[pl.ds(tp * d.rd, d.rd)]
     rfs[tp] = rfs[d.ntp + tp]
 
-    for cp in new_copies:
-        cp.wait()
     nkf = [nk[u].astype(F32) for u in range(d.steps)]
     nvf = [nv[u].astype(F32) for u in range(d.steps)]
     fresh = []
@@ -610,6 +614,8 @@
                     outs.append(sum(w * nvf[u][i : i + 1, kk * HD : (kk + 1) * HD] for u, w in enumerate(ws)))
             fresh.append([jnp.concatenate(x, axis=0) for x in (tops, totals, outs)])
 
+    p0.drain()
+    p1.drain()
     for k in range(1, d.ntp):
         source = lax.rem(tp - k + d.ntp, d.ntp)
         for cp in final(k - 1, source, tp, source):
@@ -622,19 +628,12 @@
             top = jnp.maximum(top_n, top_c)
             a, b = jnp.exp(top_n - top), jnp.exp(top_c - top)
             numer = out_n * a + rf[h, i].astype(F32) * b
-            stage[h, i] = numer / (total_n * a + total_c * b)
-    for step in range(d.steps):
-        for h in range(d.ntp):
-            for i in range(d.rd):
-                for j in range(heads):
-                    at = (h * heads + j) * HD
-                    wide[i : i + 1, at : at + HD] = stage[h, i, pl.ds(step * heads + j, 1), :]
-        out[step] = wide[...].astype(BF16)
+            result = (numer / (total_n * a + total_c * b)).astype(BF16)
+            for step in range(d.steps):
+                out[step, i, pl.ds(h * heads, heads)] = result[step * heads : (step + 1) * heads]
 
     for cp in waits:
         cp.wait_send()
-    p0.drain()
-    p1.drain()
 
 
 def make_shards(d):
@@ -658,7 +657,6 @@
             pltpu.VMEM(new_keys.shape, BF16),
             pltpu.VMEM(new_values.shape, BF16),
             pltpu.VMEM((d.ntp, rd, d.q, HD), F32),
-            pltpu.VMEM((rd, width), F32),
             pltpu.VMEM((d.ntp, rd, d.q, HD), BF16),
             pltpu.VMEM(piece_slots.shape, jnp.int32),
             pltpu.VMEM((plan_rows, 128), jnp.int32),
@@ -687,7 +685,7 @@
         ]
         result = pl.pallas_call(
             functools.partial(main_kernel, d, order),
-            out_shape=jax.ShapeDtypeStruct(queries.shape, BF16),
+            out_shape=jax.ShapeDtypeStruct((steps, rd, width // HD, HD), BF16),
             in_specs=[hbm, vmem, hbm, hbm, hbm, hbm, hbm],
             out_specs=vmem,
             scratch_shapes=scratch,
@@ -695,7 +693,7 @@
                 collective_id=0, has_side_effects=True, vmem_limit_bytes=60 * 1024 * 1024
             ),
         )(piece_slots, context_lengths.reshape(chunks, 128), queries, new_keys, new_values, key_cache, value_cache)
-        return result
+        return result.reshape(steps, rd, width)
 
     return shards
 

time: 87.5 us -> 85 us (0.971)
  Pallas kernels: 85.7 us -> 83.3 us
    pallas_call x1, Pallas kernels: 85.7 us -> 83.3 us  [shards(): pl.pallas_call(functools.partial(main_kernel, d, order), out_shape=jax.Sh...]
    unnamed x1 -> x0, local copies, waits for them, and re-layouts: 1.6 us -> none
    reshape x0 -> x1, local copies, waits for them, and re-layouts: none -> 1.56 us  [shards(): return result.reshape(steps, rd, width)]
where the time goes in v3:
time: 85 us; the launch traced here: 84.8 us
  Pallas kernels  83.3 us (98%)
  local copies, waits for them, and re-layouts  1.56 us (2%)
    pallas_call x1, Pallas kernels, shards(): pl.pallas_call(functools.partial(main_kernel, d, order), out_shape=jax.Sh...  83.3 us

profile of v3, /device:TPU:8, one launch (start us, length us, event | category | flops | bytes accessed | tf_op | source)
XLA Modules:
  0.0 84.8 jit_solution(16227019960726601825)
XLA Ops:
  0.0 83.3 %shard_map.73 = bf16[3,2,64,128]{3,2,1,0:T(8,128)(2,1)} custom-call(s32[512,128]{1,0:T(8,128)} %ps.1, s32[4,128]{1,0:T(4,128)} %bitcast.3, bf16[3,2,8192]{2,1,0:T(2,128)(2,1)} %q_in.1, bf16[3,2,1024]{2,1,0:T(2,128)(2,1)} %nk_in.1, bf16[3,2,1024]{2,1,0:T(2,128)(2,1)} %nv_in.1, bf16[40,256,256]{2,1,0:T(8,128)(2,1)} %kc.1, bf16[40,256,256]{2,1,0:T(8,128)(2,1)} %vc.1), custom_call_target="tpu_custom_call" | custom-call | tf_op jit(solution)/shard_map/pallas_call | solution.py:686
  83.3 1.6 %reshape.7 = bf16[3,2,8192]{2,1,0:T(2,128)(2,1)} reshape(bf16[3,2,64,128]{3,2,1,0:T(8,128)(2,1)} %shard_map.73) | data formatting | bytes 196608 | tf_op jit(solution)/shard_map/reshape | solution.py:696

commit v4 on v3

--- a/solution.py
+++ b/solution.py
@@ -30,7 +30,7 @@
         self.rows_of = ((0, self.split), (self.split, self.rg - self.split))
 
 
-def list_order(tasks, limit, latency=1.75, rate=95e3, tick=0.02):
+def list_order(tasks, limit, latency, rate=95e3, tick=0.02):
     left = {t[0]: t for t in tasks}
     flying = {"y": [], "z": []}
     arrived, order = {}, []
@@ -56,16 +56,19 @@
                 order.append(name)
                 busy = now + running[1]
         for axis, copies in flying.items():
+            room = rate * tick
             for c in copies:
-                c[1] -= rate * tick / len(copies)
-                if c[1] <= 0:
+                part = min(room, c[1])
+                c[1] -= part
+                room -= part
+                if c[1] <= 1e-9:
                     arrived[c[0]] = now + tick + latency
-            flying[axis] = [c for c in copies if c[1] > 0]
+            flying[axis] = [c for c in copies if c[1] > 1e-9]
         now += tick
     return order
 
 
-def gather_order(d, limit=2):
+def gather_order(d, limit=2, latency=2.0):
     tasks, depth = [], {}
 
     def hops(msg):
@@ -83,7 +86,7 @@
             add(child)
 
     add(None)
-    return list_order(tasks, limit)
+    return list_order(tasks, limit, latency)
 
 
 def gather_children(d, msg):
@@ -109,6 +112,41 @@
     return out
 
 
+def reduce_order(d, limit=2, latency=2.75):
+    tasks = []
+
+    def add(name, cost, waits, before, sends, paced, kind, ahead):
+        tasks.append((name, cost, waits, before, sends, paced, (kind, -ahead, len(tasks))))
+
+    for n, (first, second) in enumerate((("y", "z"), ("z", "y"))):
+        h1, h2, lanes = d.hops[first], d.hops[second], d.size[second]
+        size = d.rows_of[n][1] * (d.q * HD * 2 + 512)
+        for k in range(lanes):
+            last = k == lanes - 1
+            tail = 0 if last else h2[k % 2] - k // 2
+            for w in (0, 1):
+                if not h1[w]:
+                    continue
+                go = [((n, 1, w, 1, k), first, size)]
+                add(("launch", n, w, k), 0.08, [], [], go, first, 1, h1[w] + tail)
+                for j in range(1, h1[w]):
+                    ahead = h1[w] - j + tail
+                    pre = ("prebuild", n, w, j, k)
+                    add(pre, 0.06, [], [], [], None, 2, ahead)
+                    go = [((n, 1, w, j + 1, k), first, size)]
+                    add(("relay", n, w, j, k), 0.22, [(n, 1, w, j, k)], [pre], go, None, 0, ahead)
+            waits = [(n, 1, w, h1[w], k) for w in (0, 1) if h1[w]]
+            if last:
+                waits += [(n, 2, w, h2[w]) for w in (0, 1) if h2[w]]
+            elif k >= 2:
+                waits.append((n, 2, k % 2, k // 2))
+            pre = ("build", n, 0, k)
+            add(pre, 0.06, [], [], [], None, 2, tail)
+            go = [] if last else [((n, 2, k % 2, k // 2 + 1), second, size)]
+            add(("second", n, k), 0.28, waits, [pre], go, None, 0, tail)
+    return list_order(tasks, limit, latency)
+
+
 def iota(shape, dim):
     return lax.broadcasted_iota(jnp.int32, shape, dim)
 
@@ -128,21 +166,24 @@
         return jnp.sum(jnp.where(eye, jnp.broadcast_to(col, (128, 128)), 0), axis=0, keepdims=True)
 
     zero = jnp.zeros((1, 128), jnp.int32)
-    state = [[jnp.zeros((1, 1), jnp.int32), zero, zero] for _ in (0, 1)]
+    base = [jnp.zeros((1, 1), jnp.int32) for _ in (0, 1)]
+    acc = [[zero, zero, zero] for _ in (0, 1)]
+    held = {}
 
     def piece(side, c):
-        base, acc_val, acc_row = state[side]
-        owner = kv if side == 0 else partner
-        local = ps[c * 128 : (c + 1) * 128, :] - owner * d.slots
-        hit = (local >= 0) & (local < d.slots)
-        many = jnp.sum(hit.astype(jnp.int32), axis=1, keepdims=True)
-        many_row = to_row(many)
-        before = jnp.sum(jnp.where(row_in < lane, many, 0), axis=0, keepdims=True)
-        start_row = before + base
-        last = jnp.where(many_row > 0, jnp.minimum(start_row + many_row - 1, d.slots), d.slots)
-        out[5 + side * chunks + c : 6 + side * chunks + c, :] = last
-        base = base + jnp.sum(many_row, axis=1, keepdims=True)
-        start = to_col(start_row)
+        if side == 0:
+            for n, owner in enumerate((kv, partner)):
+                local = ps[c * 128 : (c + 1) * 128, :] - owner * d.slots
+                hit = (local >= 0) & (local < d.slots)
+                many = jnp.sum(hit.astype(jnp.int32), axis=1, keepdims=True)
+                before = jnp.sum(jnp.where(row_in < lane, many, 0), axis=0, keepdims=True)
+                start = to_col(before + base[n])
+                last = jnp.where(many > 0, jnp.clip(start + many - 1, 0, d.slots), d.slots)
+                out[5 + n * chunks + c : 6 + n * chunks + c, :] = to_row(last)
+                base[n] = base[n] + jnp.sum(many, axis=0, keepdims=True)
+                held[n] = (local, hit, many, start, last)
+        local, hit, many, start, _ = held[side]
+        elsewhere = held[1 - side][4]
         if side == 0:
             length = to_col(ctx[c : c + 1, :])
             left = jnp.clip(length - lane * d.slot_len, 0, d.slot_len)
@@ -150,16 +191,17 @@
             code = jnp.where(hit, lane * 32768 + local * 512 + left, far)
         for k in range(3):
             at = (lane == start + k) & (many > k)
-            acc_row += jnp.sum(jnp.where(at, row_in + c * 128, 0), axis=0, keepdims=True)
+            acc[side][1] += jnp.sum(jnp.where(at, row_in + c * 128, 0), axis=0, keepdims=True)
+            acc[side][2] += jnp.sum(jnp.where(at, elsewhere, 0), axis=0, keepdims=True)
             if side == 0:
                 first = jnp.min(code, axis=1, keepdims=True)
                 code = jnp.where(code == first, far, code)
-                acc_val += jnp.sum(jnp.where(at, lax.rem(first, 32768), 0), axis=0, keepdims=True)
-        state[side] = [base, acc_val, acc_row]
+                acc[side][0] += jnp.sum(jnp.where(at, lax.rem(first, 32768), 0), axis=0, keepdims=True)
 
     def finish():
         for side in (0, 1):
-            _, acc_val, acc_row = state[side]
+            acc_val, acc_row, other = acc[side]
+            out[5 + 2 * chunks + side : 6 + 2 * chunks + side, :] = jnp.clip(other, 0, d.slots)
             mine = lax.rem(acc_row // d.rg, 2) == core
             place = (acc_row // (2 * d.rg)) * d.rg + lax.rem(acc_row, d.rg)
             place = jnp.clip(place, 0, d.rows // 2 - 1)
@@ -179,7 +221,7 @@
 
 
 def main_kernel(
-    d, order, ps, ctx, q_in, nk_in, nv_in, kc, vc, out,
+    d, order, plan_reduce, ps, ctx, q_in, nk_in, nv_in, kc, vc, out,
     q_raw, nk, nv, stage, qx, psv, planv, meta, g, qp, qs, kb, vb, o, t, r0, r0s, r1, r1s, d0, d0s, d1, d1s, f, fs, rf, rfs,
     io_sem, kv_sem, tp_send, tp_recv, ag_send, ag_recv, fw_send, fw_recv, ex_send, ex_recv,
     s0_send, s0_recv, s1_send, s1_recv, fin_send, fin_recv,
@@ -405,7 +447,28 @@
             ref.at[0, pl.ds(0, d.slots)], ref.at[1, pl.ds(0, d.slots)], ex_send.at[n], ex_recv.at[n], partner
         ).wait_recv()
 
+    for cp in waits:
+        cp.wait_send()
+    waits.clear()
+
     lane8 = iota((8, 128), 1)
+    factors, tiles = [], {}
+    for side in (0, 1):
+        for at in range(0, d.slots, 8):
+            ids = [meta[5 + 2 * chunks + side, at + u] for u in range(8)]
+            theirs = jnp.concatenate([t[1 - side, pl.ds(i, 1), :] for i in ids], axis=0)
+            mine = t[side, pl.ds(at, 8), :]
+            top = jnp.maximum(mine, theirs)
+            factor = jnp.exp(mine - top)
+            factors.append(factor)
+            tiles[side, at] = jnp.where(lane8 < 64, top, mine * pltpu.roll(factor, 64, 1))
+    cols = jnp.transpose(jnp.concatenate(factors, axis=0))
+    for (side, at), tile in tiles.items():
+        t[side, pl.ds(at, 8), :] = tile
+    for side in (0, 1):
+        for i in range(d.slots):
+            n = side * d.slots + i
+            o[side, i] = (o[side, i].astype(F32) * cols[: d.q, n : n + 1]).astype(BF16)
 
     def pad8(x):
         if x.shape[0] == 8:
@@ -483,50 +546,41 @@
         def lane(self, k):
             return (self.h2[0] + ((k + 1) // 2) * (1 if k % 2 else -1)) % self.lanes
 
-        def build(self, offsets, k):
+        def build(self, o1, k):
             lane = self.lane(k)
-            jobs = []
-            for o1 in offsets:
-                oy, oz = (o1, lane) if self.first == "y" else (lane, o1)
-                kv_to = kv_at(oy, oz)
-                line, col = lax.div(kv_to, per_row), lax.rem(kv_to, per_row) * d.rg + self.start
-                ids, stats = [], []
-                for side in (0, 1):
-                    ids.append([meta[5 + side * chunks + line, col + r] for r in range(self.count)])
-                    stats.append(
-                        pad8(jnp.concatenate([t[side, pl.ds(i, 1), :] for i in ids[side]], axis=0))
-                    )
-                jobs.append((ids, stats, self.chip_sum(o1, lane)))
-            ready = [prepare(stats, self.count) for _, stats, _ in jobs]
-            for (ids, _, dst), (tile, cols) in zip(jobs, ready):
-                apply(tile, cols, lambda k, r: o[k, ids[k][r]], 2, self.count, *dst)
-
-        def launch(self, k):
-            ways = [way for way in (0, 1) if self.h1[way]]
-            far = [(1 - 2 * way) * self.h1[way] for way in ways]
-            self.build(far, k)
+            oy, oz = (o1, lane) if self.first == "y" else (lane, o1)
+            kv_to = kv_at(oy, oz)
+            line, col = lax.div(kv_to, per_row), lax.rem(kv_to, per_row) * d.rg + self.start
+            ids = [
+                [meta[5 + side * chunks + line, col + r] for r in range(self.count)] for side in (0, 1)
+            ]
+            stats = [
+                jnp.concatenate([t[side, pl.ds(i, 1), :] for i in ids[side]], axis=0) for side in (0, 1)
+            ]
+            dst, dst_s = self.chip_sum(o1, lane)
+            dst_s[...] = jnp.where(
+                lane8[: self.count] < 64, jnp.maximum(stats[0], stats[1]), stats[0] + stats[1]
+            )
+            for r in range(self.count):
+                dst[r] = o[0, ids[0][r]] + o[1, ids[1][r]]
+
+        def launch(self, way, k):
+            o1 = (1 - 2 * way) * self.h1[way]
+            self.build(o1, k)
             lane = self.lane(k)
-            for way, o1 in zip(ways, far):
-                self.send(self.chip_sum(o1, lane), self.id1(way, 1, lane), self.first, way)
-
-        def rest(self, k):
-            for j in range(1, self.h1[0]):
-                ways = [way for way in (0, 1) if j < self.h1[way]]
-                self.build([(1 - 2 * way) * (self.h1[way] - j) for way in ways], k)
-            self.build([0], k)
-
-        def relay(self, j, k):
+            self.send(self.chip_sum(o1, lane), self.id1(way, 1, lane), self.first, way)
+
+        def prebuild(self, way, j, k):
+            self.build((1 - 2 * way) * (self.h1[way] - j), k)
+
+        def relay(self, way, j, k):
             lane = self.lane(k)
-            ways = [way for way in (0, 1) if j < self.h1[way]]
-            jobs = []
-            for way in ways:
-                n = self.id1(way, j, lane)
-                self.wait(n)
-                left = (1 - 2 * way) * (self.h1[way] - j)
-                jobs.append(([self.bufs(n), self.chip_sum(left, lane)], self.bufs(n)))
-            merge(jobs, self.count)
-            for way, (_, src) in zip(ways, jobs):
-                self.send(src, self.id1(way, j + 1, lane), self.first, way)
+            n = self.id1(way, j, lane)
+            self.wait(n)
+            left = (1 - 2 * way) * (self.h1[way] - j)
+            src = self.bufs(n)
+            merge([([src, self.chip_sum(left, lane)], src)], self.count)
+            self.send(src, self.id1(way, j + 1, lane), self.first, way)
 
         def second_step(self, k, result):
             lane = self.lane(k)
@@ -556,20 +610,12 @@
     fin0 = (f.at[pl.ds(p0.start, p0.count)], fs.at[pl.ds(p0.start, p0.count)])
     fin1 = (f.at[pl.ds(p1.start, p1.count)], fs.at[pl.ds(p1.start, p1.count)])
 
-    lag = 2
-    steps = []
-    for n, (p, fin) in enumerate(((p1, fin1), (p0, fin0))):
-        last = p.lanes - 1
-        for k in range(p.lanes):
-            steps.append((k, 4, n, functools.partial(p.launch, k)))
-            steps.append((k, 5, n, functools.partial(p.rest, k)))
-            for j in range(1, p.h1[0]):
-                steps.append((k + lag * j, 1, n, functools.partial(p.relay, j, k)))
-            late = lag * p.h1[0] + k + (lag - 1 if k == last else 0)
-            steps.append((late, 3, n, functools.partial(p.second_step, k, fin)))
-    steps.sort(key=lambda x: x[:3])
-    for _, _, _, run in steps:
-        run()
+    parts, fins = (p0, p1), (fin0, fin1)
+    for what, n, *rest in plan_reduce:
+        if what == "second":
+            parts[n].second_step(*rest, fins[n])
+        else:
+            getattr(parts[n], what)(*rest)
 
     for n in range(d.ntp):
         for i in range(d.rd):
@@ -638,6 +684,7 @@
 
 def make_shards(d):
     order = gather_order(d)
+    plan_reduce = reduce_order(d)
 
     def shards(queries, new_keys, new_values, key_cache, value_cache, context_lengths, piece_slots):
         steps, rd, width = queries.shape
@@ -651,7 +698,7 @@
         dma = pltpu.SemaphoreType.DMA
         sem = lambda *shape: dma(shape)
         nt = max(d.ntp - 1, 1)
-        plan_rows = -(-(5 + 2 * chunks) // 8) * 8
+        plan_rows = -(-(7 + 2 * chunks) // 8) * 8
         scratch = [
             pltpu.VMEM(queries.shape, BF16),
             pltpu.VMEM(new_keys.shape, BF16),
@@ -684,7 +731,7 @@
             sem(2), sem(2), sem(2, n0), sem(2, n0), sem(2, n1), sem(2, n1), sem(2, nt), sem(2, nt),
         ]
         result = pl.pallas_call(
-            functools.partial(main_kernel, d, order),
+            functools.partial(main_kernel, d, order, plan_reduce),
             out_shape=jax.ShapeDtypeStruct((steps, rd, width // HD, HD), BF16),
             in_specs=[hbm, vmem, hbm, hbm, hbm, hbm, hbm],
             out_specs=vmem,

time: 85 us -> 81.5 us (0.959)
  Pallas kernels: 83.3 us -> 79.5 us
    pallas_call x1, Pallas kernels: 83.3 us -> 79.5 us  [shards(): pl.pallas_call(functools.partial(main_kernel, d, order, plan_reduce), out...]
where the time goes in v4:
time: 81.5 us; the launch traced here: 81.1 us
  Pallas kernels  79.5 us (98%)
  local copies, waits for them, and re-layouts  1.56 us (2%)
    pallas_call x1, Pallas kernels, shards(): pl.pallas_call(functools.partial(main_kernel, d, order, plan_reduce), out...  79.5 us

profile of v4, /device:TPU:8, one launch (start us, length us, event | category | flops | bytes accessed | tf_op | source)
XLA Modules:
  0.0 81.1 jit_solution(6182352112624550196)
XLA Ops:
  0.0 79.5 %shard_map.73 = bf16[3,2,64,128]{3,2,1,0:T(8,128)(2,1)} custom-call(s32[512,128]{1,0:T(8,128)} %ps.1, s32[4,128]{1,0:T(4,128)} %bitcast.3, bf16[3,2,8192]{2,1,0:T(2,128)(2,1)} %q_in.1, bf16[3,2,1024]{2,1,0:T(2,128)(2,1)} %nk_in.1, bf16[3,2,1024]{2,1,0:T(2,128)(2,1)} %nv_in.1, bf16[40,256,256]{2,1,0:T(8,128)(2,1)} %kc.1, bf16[40,256,256]{2,1,0:T(8,128)(2,1)} %vc.1), custom_call_target="tpu_custom_call" | custom-call | tf_op jit(solution)/shard_map/pallas_call | solution.py:733
  79.5 1.6 %reshape.7 = bf16[3,2,8192]{2,1,0:T(2,128)(2,1)} reshape(bf16[3,2,64,128]{3,2,1,0:T(8,128)(2,1)} %shard_map.73) | data formatting | bytes 196608 | tf_op jit(solution)/shard_map/reshape | solution.py:743

commit v5 on v4

--- a/solution.py
+++ b/solution.py
@@ -222,7 +222,7 @@
 
 def main_kernel(
     d, order, plan_reduce, ps, ctx, q_in, nk_in, nv_in, kc, vc, out,
-    q_raw, nk, nv, stage, qx, psv, planv, meta, g, qp, qs, kb, vb, o, t, r0, r0s, r1, r1s, d0, d0s, d1, d1s, f, fs, rf, rfs,
+    q_raw, nk, nv, stage, fresh, qx, psv, planv, meta, g, qp, qs, kb, vb, o, t, r0, r0s, r1, r1s, d0, d0s, d1, d1s, f, fs, rf, rfs,
     io_sem, kv_sem, tp_send, tp_recv, ag_send, ag_recv, fw_send, fw_recv, ex_send, ex_recv,
     s0_send, s0_recv, s1_send, s1_recv, fin_send, fin_recv,
 ):
@@ -363,20 +363,25 @@
         plan_copy.start()
     plan_copy.wait()
 
-    def pick(i, c):
-        for u in range(4):
-            qs[4 * i + u] = g[meta[4, 4 * i + u]]
+    unroll = 8
+
+    def chunk(src, dst, send, recv, n):
+        at = pl.ds(n * unroll, unroll)
+        return remote(src.at[at], dst.at[at], send.at[n], recv.at[n], partner)
+
+    def pick(n, c):
+        for u in range(unroll):
+            qs[n * unroll + u] = g[meta[4, n * unroll + u]]
+        chunk(qs, qp, fw_send, fw_recv, n).start()
         return c
 
-    lax.fori_loop(0, d.slots // 4, pick, 0)
-    cp = remote(qs, qp, fw_send.at[0], fw_recv.at[0], partner)
-    cp.start()
+    chunks_of_slots = d.slots // unroll
+    lax.fori_loop(0, chunks_of_slots, pick, 0)
     for copy in kv_copies + new_copies:
         copy.wait()
     for other in waits:
         other.wait_send()
     waits.clear()
-    cp.wait()
 
     head = lax.rem(iota((d.q, 128), 0) // d.group, d.kvl)
     head_masks = [(head == k).astype(F32).astype(BF16) for k in range(d.kvl)]
@@ -384,14 +389,13 @@
     lane_slot = iota((d.q, d.slot_len), 1)
     scale = 1.0 / math.sqrt(HD)
 
-    unroll = 8
-
     def attend_many(it, carry):
+        chunk(qs, qp, fw_send, fw_recv, it).wait_recv()
         m_p, l_p, o_p, mc, lc = carry
         at = [it * unroll + u for u in range(unroll)]
         rows = [meta[0, i] for i in at]
-        qs = [jnp.where(row >= 0, g[jnp.maximum(row, 0)], qp[i]) for row, i in zip(rows, at)]
-        q2 = [jnp.concatenate([q * mask for mask in head_masks], axis=1) for q in qs]
+        q1 = [jnp.where(row >= 0, g[jnp.maximum(row, 0)], qp[i]) for row, i in zip(rows, at)]
+        q2 = [jnp.concatenate([q * mask for mask in head_masks], axis=1) for q in q1]
         slots = [meta[1, i] for i in at]
         score = [
             lax.dot_general(q, kb[slot], (((1,), (1,)), ((), ())), preferred_element_type=F32)
@@ -418,6 +422,7 @@
             lc = jnp.where(lane128 == i, l_p, lc)
         for u, i in enumerate(at):
             o[0, i] = accs[u]
+        chunk(o.at[0], o.at[1], ex_send, ex_recv, it).start()
         return m_p, l_p, o_p, mc, lc
 
     zero_col = jnp.zeros((d.q, 1), F32)
@@ -436,20 +441,46 @@
         t[side, pl.ds(d.slots, spare)] = nobody
         o[side, d.slots] = jnp.zeros((d.q, 128), BF16)
 
-    for n, ref in enumerate((o, t)):
-        cp = remote(
-            ref.at[0, pl.ds(0, d.slots)], ref.at[1, pl.ds(0, d.slots)], ex_send.at[n], ex_recv.at[n], partner
-        )
-        cp.start()
-        waits.append(cp)
-    for n, ref in enumerate((o, t)):
-        remote(
-            ref.at[0, pl.ds(0, d.slots)], ref.at[1, pl.ds(0, d.slots)], ex_send.at[n], ex_recv.at[n], partner
-        ).wait_recv()
-
-    for cp in waits:
-        cp.wait_send()
-    waits.clear()
+    table_copy = remote(
+        t.at[0, pl.ds(0, d.slots)],
+        t.at[1, pl.ds(0, d.slots)],
+        ex_send.at[chunks_of_slots],
+        ex_recv.at[chunks_of_slots],
+        partner,
+    )
+    table_copy.start()
+
+    nkf = [nk[u].astype(F32) for u in range(d.steps)]
+    nvf = [nv[u].astype(F32) for u in range(d.steps)]
+    for h in range(d.ntp):
+        for i in range(d.rd):
+            tops, totals, outs = [], [], []
+            qf = qx[h, i].astype(F32)
+            for step in range(d.steps):
+                for k in range(d.kvl):
+                    at = (step * d.kvl + k) * d.group
+                    kk = h * d.kvl + k
+                    q_k = qf[at : at + d.group]
+                    scores = [
+                        jnp.sum(q_k * nkf[u][i : i + 1, kk * HD : (kk + 1) * HD], axis=1, keepdims=True) * scale
+                        for u in range(step + 1)
+                    ]
+                    top = functools.reduce(jnp.maximum, scores)
+                    ws = [jnp.exp(x - top) for x in scores]
+                    tops.append(top)
+                    totals.append(sum(ws))
+                    outs.append(sum(w * nvf[u][i : i + 1, kk * HD : (kk + 1) * HD] for u, w in enumerate(ws)))
+            for n, x in enumerate((tops, totals)):
+                fresh[h, i, n] = jnp.broadcast_to(jnp.concatenate(x, axis=0), (d.q, 128))
+            stage[h, i] = jnp.concatenate(outs, axis=0)
+
+    def exchanged(n, c):
+        chunk(qs, qp, fw_send, fw_recv, n).wait_send()
+        chunk(o.at[0], o.at[1], ex_send, ex_recv, n).wait()
+        return c
+
+    lax.fori_loop(0, chunks_of_slots, exchanged, 0)
+    table_copy.wait()
 
     lane8 = iota((8, 128), 1)
     factors, tiles = [], {}
@@ -637,29 +668,6 @@
     rf[tp] = f[pl.ds(tp * d.rd, d.rd)]
     rfs[tp] = rfs[d.ntp + tp]
 
-    nkf = [nk[u].astype(F32) for u in range(d.steps)]
-    nvf = [nv[u].astype(F32) for u in range(d.steps)]
-    fresh = []
-    for h in range(d.ntp):
-        for i in range(d.rd):
-            tops, totals, outs = [], [], []
-            qf = qx[h, i].astype(F32)
-            for step in range(d.steps):
-                for k in range(d.kvl):
-                    at = (step * d.kvl + k) * d.group
-                    kk = h * d.kvl + k
-                    qs = qf[at : at + d.group]
-                    scores = [
-                        jnp.sum(qs * nkf[u][i : i + 1, kk * HD : (kk + 1) * HD], axis=1, keepdims=True) * scale
-                        for u in range(step + 1)
-                    ]
-                    top = functools.reduce(jnp.maximum, scores)
-                    ws = [jnp.exp(x - top) for x in scores]
-                    tops.append(top)
-                    totals.append(sum(ws))
-                    outs.append(sum(w * nvf[u][i : i + 1, kk * HD : (kk + 1) * HD] for u, w in enumerate(ws)))
-            fresh.append([jnp.concatenate(x, axis=0) for x in (tops, totals, outs)])
-
     p0.drain()
     p1.drain()
     for k in range(1, d.ntp):
@@ -669,7 +677,7 @@
     for h in range(d.ntp):
         cols = jnp.transpose(pad8(rfs[h]))
         for i in range(d.rd):
-            top_n, total_n, out_n = fresh[h * d.rd + i]
+            top_n, total_n, out_n = fresh[h, i, 0], fresh[h, i, 1], stage[h, i]
             top_c, total_c = cols[: d.q, i : i + 1], cols[64 : 64 + d.q, i : i + 1]
             top = jnp.maximum(top_n, top_c)
             a, b = jnp.exp(top_n - top), jnp.exp(top_c - top)
@@ -704,6 +712,7 @@
             pltpu.VMEM(new_keys.shape, BF16),
             pltpu.VMEM(new_values.shape, BF16),
             pltpu.VMEM((d.ntp, rd, d.q, HD), F32),
+            pltpu.VMEM((d.ntp, rd, 2, d.q, 128), F32),
             pltpu.VMEM((d.ntp, rd, d.q, HD), BF16),
             pltpu.VMEM(piece_slots.shape, jnp.int32),
             pltpu.VMEM((plan_rows, 128), jnp.int32),
@@ -727,8 +736,8 @@
             pltpu.VMEM((d.rg, 128), F32),
             pltpu.VMEM((d.ntp, rd, d.q, HD), BF16),
             pltpu.VMEM((2 * d.ntp, rd, 128), F32),
-            sem(5), sem(2, 4), sem(nt), sem(nt), sem(len(order) // 2), sem(len(order) // 2), sem(1), sem(1),
-            sem(2), sem(2), sem(2, n0), sem(2, n0), sem(2, n1), sem(2, n1), sem(2, nt), sem(2, nt),
+            sem(5), sem(2, 4), sem(nt), sem(nt), sem(len(order) // 2), sem(len(order) // 2), sem(d.slots // 8), sem(d.slots // 8),
+            sem(d.slots // 8 + 1), sem(d.slots // 8 + 1), sem(2, n0), sem(2, n0), sem(2, n1), sem(2, n1), sem(2, nt), sem(2, nt),
         ]
         result = pl.pallas_call(
             functools.partial(main_kernel, d, order, plan_reduce),

time: 81.5 us -> 79.9 us (0.980)
  Pallas kernels: 79.5 us -> 77.8 us
    pallas_call x1, Pallas kernels: 79.5 us -> 77.8 us  [shards(): pl.pallas_call(functools.partial(main_kernel, d, order, plan_reduce), out...]
where the time goes in v5:
time: 79.9 us; the launch traced here: 79.4 us
  Pallas kernels  77.8 us (97%)
  local copies, waits for them, and re-layouts  1.56 us (2%)
    pallas_call x1, Pallas kernels, shards(): pl.pallas_call(functools.partial(main_kernel, d, order, plan_reduce), out...  77.8 us

profile of v5, /device:TPU:8, one launch (start us, length us, event | category | flops | bytes accessed | tf_op | source)
XLA Modules:
  0.0 79.4 jit_solution(16978738151021384204)
XLA Ops:
  0.0 77.8 %shard_map.73 = bf16[3,2,64,128]{3,2,1,0:T(8,128)(2,1)} custom-call(s32[512,128]{1,0:T(8,128)} %ps.1, s32[4,128]{1,0:T(4,128)} %bitcast.3, bf16[3,2,8192]{2,1,0:T(2,128)(2,1)} %q_in.1, bf16[3,2,1024]{2,1,0:T(2,128)(2,1)} %nk_in.1, bf16[3,2,1024]{2,1,0:T(2,128)(2,1)} %nv_in.1, bf16[40,256,256]{2,1,0:T(8,128)(2,1)} %kc.1, bf16[40,256,256]{2,1,0:T(8,128)(2,1)} %vc.1), custom_call_target="tpu_custom_call" | custom-call | tf_op jit(solution)/shard_map/pallas_call | solution.py:742
  77.8 1.6 %reshape.7 = bf16[3,2,8192]{2,1,0:T(2,128)(2,1)} reshape(bf16[3,2,64,128]{3,2,1,0:T(8,128)(2,1)} %shard_map.73) | data formatting | bytes 196608 | tf_op jit(solution)/shard_map/reshape | solution.py:752

commit v6 on v5

--- a/solution.py
+++ b/solution.py
@@ -221,15 +221,15 @@
 
 
 def main_kernel(
-    d, order, plan_reduce, ps, ctx, q_in, nk_in, nv_in, kc, vc, out,
-    q_raw, nk, nv, stage, fresh, qx, psv, planv, meta, g, qp, qs, kb, vb, o, t, r0, r0s, r1, r1s, d0, d0s, d1, d1s, f, fs, rf, rfs,
+    d, order, plan_reduce, ps, ctx, q_raw, nk, nv, kc, vc, out,
+    stage, fresh, qx, planv, meta, g, qp, qs, kb, vb, o, t, r0, r0s, r1, r1s, d0, d0s, d1, d1s, f, fs, rf, rfs,
     io_sem, kv_sem, tp_send, tp_recv, ag_send, ag_recv, fw_send, fw_recv, ex_send, ex_recv,
     s0_send, s0_recv, s1_send, s1_recv, fin_send, fin_recv,
 ):
     kv = lax.axis_index("kv")
     tp = lax.axis_index("tp")
     core = lax.rem(kv, 2)
-    sgn = 1 - 2 * core
+    sgn = 2 * core - 1
     chip = kv // 2
     pos = {"y": chip // d.nz, "z": lax.rem(chip, d.nz)}
 
@@ -250,7 +250,7 @@
     def neighbour(axis, step):
         return (kv_at(step, 0) if axis == "y" else kv_at(0, step), tp)
 
-    partner = (kv + sgn, tp)
+    partner = (kv + 1 - 2 * core, tp)
 
     def remote(src, dst, ss, rs, dev):
         return pltpu.make_async_remote_copy(
@@ -259,16 +259,6 @@
 
     chunks = d.rows // 128
 
-    q_copy = pltpu.make_async_copy(q_in, q_raw, io_sem.at[2])
-    q_copy.start()
-    new_copies = [
-        pltpu.make_async_copy(src, dst, io_sem.at[n])
-        for n, (src, dst) in enumerate(((nk_in, nk), (nv_in, nv)), 3)
-    ]
-    for cp in new_copies:
-        cp.start()
-    ps_copy = pltpu.make_async_copy(ps, psv, io_sem.at[0])
-    ps_copy.start()
     parts_kv = kv_sem.shape[1]
     per = d.slots // parts_kv
     kv_copies = []
@@ -291,7 +281,6 @@
     for dev in friends:
         pl.semaphore_signal(barrier, inc=1, device_id=dev, device_id_type=MESH)
 
-    q_copy.wait()
     heads = d.kvl * d.group
     for step in range(d.steps):
         q_step = q_raw[step].astype(F32)
@@ -342,10 +331,9 @@
         cp.start()
         waits.append(cp)
 
-    ps_copy.wait()
     pieces = []
-    slot_plan(d, kv, psv, ctx, planv, pieces)
-    plan_copy = pltpu.make_async_copy(planv, meta, io_sem.at[1])
+    slot_plan(d, kv, ps, ctx, planv, pieces)
+    plan_copy = pltpu.make_async_copy(planv, meta, io_sem.at[0])
     for place_in, (what, msg) in enumerate(order):
         if what == "send":
             ship(msg)
@@ -377,7 +365,7 @@
 
     chunks_of_slots = d.slots // unroll
     lax.fori_loop(0, chunks_of_slots, pick, 0)
-    for copy in kv_copies + new_copies:
+    for copy in kv_copies:
         copy.wait()
     for other in waits:
         other.wait_send()
@@ -708,13 +696,9 @@
         nt = max(d.ntp - 1, 1)
         plan_rows = -(-(7 + 2 * chunks) // 8) * 8
         scratch = [
-            pltpu.VMEM(queries.shape, BF16),
-            pltpu.VMEM(new_keys.shape, BF16),
-            pltpu.VMEM(new_values.shape, BF16),
             pltpu.VMEM((d.ntp, rd, d.q, HD), F32),
             pltpu.VMEM((d.ntp, rd, 2, d.q, 128), F32),
             pltpu.VMEM((d.ntp, rd, d.q, HD), BF16),
-            pltpu.VMEM(piece_slots.shape, jnp.int32),
             pltpu.VMEM((plan_rows, 128), jnp.int32),
             pltpu.SMEM((plan_rows, 128), jnp.int32),
             pltpu.VMEM((d.rows // 2, d.q, HD), BF16),
@@ -736,17 +720,17 @@
             pltpu.VMEM((d.rg, 128), F32),
             pltpu.VMEM((d.ntp, rd, d.q, HD), BF16),
             pltpu.VMEM((2 * d.ntp, rd, 128), F32),
-            sem(5), sem(2, 4), sem(nt), sem(nt), sem(len(order) // 2), sem(len(order) // 2), sem(d.slots // 8), sem(d.slots // 8),
+            sem(1), sem(2, 4), sem(nt), sem(nt), sem(len(order) // 2), sem(len(order) // 2), sem(d.slots // 8), sem(d.slots // 8),
             sem(d.slots // 8 + 1), sem(d.slots // 8 + 1), sem(2, n0), sem(2, n0), sem(2, n1), sem(2, n1), sem(2, nt), sem(2, nt),
         ]
         result = pl.pallas_call(
             functools.partial(main_kernel, d, order, plan_reduce),
             out_shape=jax.ShapeDtypeStruct((steps, rd, width // HD, HD), BF16),
-            in_specs=[hbm, vmem, hbm, hbm, hbm, hbm, hbm],
+            in_specs=[vmem, vmem, vmem, vmem, vmem, hbm, hbm],
             out_specs=vmem,
             scratch_shapes=scratch,
             compiler_params=pltpu.CompilerParams(
-                collective_id=0, has_side_effects=True, vmem_limit_bytes=60 * 1024 * 1024
+                collective_id=0, has_side_effects=True, vmem_limit_bytes=52 * 1024 * 1024
             ),
         )(piece_slots, context_lengths.reshape(chunks, 128), queries, new_keys, new_values, key_cache, value_cache)
         return result.reshape(steps, rd, width)

time: 79.9 us -> 80.4 us (level)
  local copies, waits for them, and re-layouts: 1.56 us -> 4.6 us
  Pallas kernels: 77.8 us -> 75.3 us
    unnamed x0 -> x10, local copies, waits for them, and re-layouts: none -> 3.94 us
    pallas_call x1, Pallas kernels: 77.8 us -> 75.3 us  [shards(): pl.pallas_call(functools.partial(main_kernel, d, order, plan_reduce), out...]
    reshape x1, local copies, waits for them, and re-layouts: 1.56 us -> 0.67 us  [shards(): return result.reshape(steps, rd, width)]
where the time goes in v6:
time: 80.4 us; the launch traced here: 80 us
  Pallas kernels  75.3 us (94%)
  local copies, waits for them, and re-layouts  4.6 us (6%)
    pallas_call x1, Pallas kernels, shards(): pl.pallas_call(functools.partial(main_kernel, d, order, plan_reduce), out...  75.3 us
    unnamed x10, local copies, waits for them, and re-layouts  3.94 us

profile of v6, /device:TPU:8, one launch (start us, length us, event | category | flops | bytes accessed | tf_op | source)
XLA Modules:
  0.0 80.0 jit_solution(3256329912475628550)
XLA Ops:
  0.0 0.0 copy-start
  0.0 0.9 %copy-done = s32[512,128]{1,0:T(8,128)S(1)} copy-done((s32[512,128]{1,0:T(8,128)S(1)}, s32[512,128]{1,0:T(8,128)}, u32[]{:S(2)}) %copy-start) | copy-done | bytes 262168
  1.0 0.0 copy-start.1
  1.0 0.9 %copy-done.1 = bf16[3,2,8192]{2,1,0:T(2,128)(2,1)S(1)} copy-done((bf16[3,2,8192]{2,1,0:T(2,128)(2,1)S(1)}, bf16[3,2,8192]{2,1,0:T(2,128)(2,1)}, u32[]{:S(2)}) %copy-start.1) | copy-done | bytes 98328
  1.8 0.0 copy-start.2
  1.8 0.7 copy-done.2
  2.6 0.0 copy-start.3
  2.6 0.7 copy-done.3
  3.3 0.0 copy-start.4
  3.3 0.7 copy-done.4
  3.9 75.3 %shard_map.73 = bf16[3,2,64,128]{3,2,1,0:T(8,128)(2,1)S(1)} custom-call(s32[512,128]{1,0:T(8,128)S(1)} %copy-done, s32[4,128]{1,0:T(4,128)S(1)} %bitcast.3, bf16[3,2,8192]{2,1,0:T(2,128)(2,1)S(1)} %copy-done.1, bf16[3,2,1024]{2,1,0:T(2,128)(2,1)S(1)} %copy-done.2, bf16[3,2,1024]{2,1,0:T(2,128)(2,1)S(1)} %copy-done.3, bf16[40,256,256]{2,1,0:T(8,128)(2,1)} %kc.1, ...), custom_call_target="tpu_custom_call" | custom-call | tf_op jit(solution)/shard_map/pallas_call | solution.py:726
  79.3 0.7 reshape.7
Async XLA Ops:
  0.0 0.9 %copy-start = (s32[512,128]{1,0:T(8,128)S(1)}, s32[512,128]{1,0:T(8,128)}, u32[]{:S(2)}) copy-start(s32[512,128]{1,0:T(8,128)} %ps.1) | copy-start | bytes 786436
  1.0 0.9 %copy-start.1 = (bf16[3,2,8192]{2,1,0:T(2,128)(2,1)S(1)}, bf16[3,2,8192]{2,1,0:T(2,128)(2,1)}, u32[]{:S(2)}) copy-start(bf16[3,2,8192]{2,1,0:T(2,128)(2,1)} %q_raw.1) | copy-start | bytes 294916
  1.8 0.7 copy-start.2
  2.6 0.7 copy-start.3
  3.3 0.7 copy-start.4

commit v7 on v5

--- a/solution.py
+++ b/solution.py
@@ -221,15 +221,15 @@
 
 
 def main_kernel(
-    d, order, plan_reduce, ps, ctx, q_in, nk_in, nv_in, kc, vc, out,
-    q_raw, nk, nv, stage, fresh, qx, psv, planv, meta, g, qp, qs, kb, vb, o, t, r0, r0s, r1, r1s, d0, d0s, d1, d1s, f, fs, rf, rfs,
+    d, order, plan_reduce, ps, ctx_in, q_in, nk_in, nv_in, kc, vc, out,
+    ctx, q_raw, nk, nv, stage, fresh, qx, psv, planv, meta, g, qp, qs, kb, vb, o, t, r0, r0s, r1, r1s, d0, d0s, d1, d1s, f, fs, rf, rfs,
     io_sem, kv_sem, tp_send, tp_recv, ag_send, ag_recv, fw_send, fw_recv, ex_send, ex_recv,
     s0_send, s0_recv, s1_send, s1_recv, fin_send, fin_recv,
 ):
     kv = lax.axis_index("kv")
     tp = lax.axis_index("tp")
     core = lax.rem(kv, 2)
-    sgn = 1 - 2 * core
+    sgn = 2 * core - 1
     chip = kv // 2
     pos = {"y": chip // d.nz, "z": lax.rem(chip, d.nz)}
 
@@ -250,7 +250,7 @@
     def neighbour(axis, step):
         return (kv_at(step, 0) if axis == "y" else kv_at(0, step), tp)
 
-    partner = (kv + sgn, tp)
+    partner = (kv + 1 - 2 * core, tp)
 
     def remote(src, dst, ss, rs, dev):
         return pltpu.make_async_remote_copy(
@@ -263,7 +263,7 @@
     q_copy.start()
     new_copies = [
         pltpu.make_async_copy(src, dst, io_sem.at[n])
-        for n, (src, dst) in enumerate(((nk_in, nk), (nv_in, nv)), 3)
+        for n, (src, dst) in enumerate(((nk_in, nk), (nv_in, nv), (ctx_in, ctx)), 3)
     ]
     for cp in new_copies:
         cp.start()
@@ -343,6 +343,7 @@
         waits.append(cp)
 
     ps_copy.wait()
+    new_copies.pop().wait()
     pieces = []
     slot_plan(d, kv, psv, ctx, planv, pieces)
     plan_copy = pltpu.make_async_copy(planv, meta, io_sem.at[1])
@@ -708,6 +709,7 @@
         nt = max(d.ntp - 1, 1)
         plan_rows = -(-(7 + 2 * chunks) // 8) * 8
         scratch = [
+            pltpu.VMEM((chunks, 128), jnp.int32),
             pltpu.VMEM(queries.shape, BF16),
             pltpu.VMEM(new_keys.shape, BF16),
             pltpu.VMEM(new_values.shape, BF16),
@@ -736,17 +738,17 @@
             pltpu.VMEM((d.rg, 128), F32),
             pltpu.VMEM((d.ntp, rd, d.q, HD), BF16),
             pltpu.VMEM((2 * d.ntp, rd, 128), F32),
-            sem(5), sem(2, 4), sem(nt), sem(nt), sem(len(order) // 2), sem(len(order) // 2), sem(d.slots // 8), sem(d.slots // 8),
+            sem(6), sem(2, 4), sem(nt), sem(nt), sem(len(order) // 2), sem(len(order) // 2), sem(d.slots // 8), sem(d.slots // 8),
             sem(d.slots // 8 + 1), sem(d.slots // 8 + 1), sem(2, n0), sem(2, n0), sem(2, n1), sem(2, n1), sem(2, nt), sem(2, nt),
         ]
         result = pl.pallas_call(
             functools.partial(main_kernel, d, order, plan_reduce),
-            out_shape=jax.ShapeDtypeStruct((steps, rd, width // HD, HD), BF16),
-            in_specs=[hbm, vmem, hbm, hbm, hbm, hbm, hbm],
+            out_shape=pltpu.VMEM((steps, rd, width // HD, HD), BF16),
+            in_specs=[hbm] * 7,
             out_specs=vmem,
             scratch_shapes=scratch,
             compiler_params=pltpu.CompilerParams(
-                collective_id=0, has_side_effects=True, vmem_limit_bytes=60 * 1024 * 1024
+                collective_id=0, has_side_effects=True, vmem_limit_bytes=56 * 1024 * 1024
             ),
         )(piece_slots, context_lengths.reshape(chunks, 128), queries, new_keys, new_values, key_cache, value_cache)
         return result.reshape(steps, rd, width)

time: 79.9 us -> 76.2 us (0.954)
  Pallas kernels: 77.8 us -> 75.3 us
  local copies, waits for them, and re-layouts: 1.56 us -> 0.67 us
    pallas_call x1, Pallas kernels: 77.8 us -> 75.3 us  [shards(): pl.pallas_call(functools.partial(main_kernel, d, order, plan_reduce), out...]
    reshape x1, local copies, waits for them, and re-layouts: 1.56 us -> 0.67 us  [shards(): return result.reshape(steps, rd, width)]
where the time goes in v7:
time: 76.2 us; the launch traced here: 75.9 us
  Pallas kernels  75.3 us (99%)
    pallas_call x1, Pallas kernels, shards(): pl.pallas_call(functools.partial(main_kernel, d, order, plan_reduce), out...  75.3 us

profile of v7, /device:TPU:8, one launch (start us, length us, event | category | flops | bytes accessed | tf_op | source)
XLA Modules:
  0.0 75.9 jit_solution(1090190617175218029)
XLA Ops:
  0.0 75.3 %shard_map.73 = bf16[3,2,64,128]{3,2,1,0:T(8,128)(2,1)S(1)} custom-call(s32[512,128]{1,0:T(8,128)} %ps.1, s32[4,128]{1,0:T(4,128)} %bitcast.3, bf16[3,2,8192]{2,1,0:T(2,128)(2,1)} %q_in.1, bf16[3,2,1024]{2,1,0:T(2,128)(2,1)} %nk_in.1, bf16[3,2,1024]{2,1,0:T(2,128)(2,1)} %nv_in.1, bf16[40,256,256]{2,1,0:T(8,128)(2,1)} %kc.1, bf16[40,256,256]{2,1,0:T(8,128)(2,1)} %vc.1), custom_call_target="tpu_custom_call" | custom-call | tf_op jit(solution)/shard_map/pallas_call | solution.py:744
  75.3 0.7 reshape.7

commit v8 on v7

--- a/solution.py
+++ b/solution.py
@@ -261,25 +261,6 @@
 
     q_copy = pltpu.make_async_copy(q_in, q_raw, io_sem.at[2])
     q_copy.start()
-    new_copies = [
-        pltpu.make_async_copy(src, dst, io_sem.at[n])
-        for n, (src, dst) in enumerate(((nk_in, nk), (nv_in, nv), (ctx_in, ctx)), 3)
-    ]
-    for cp in new_copies:
-        cp.start()
-    ps_copy = pltpu.make_async_copy(ps, psv, io_sem.at[0])
-    ps_copy.start()
-    parts_kv = kv_sem.shape[1]
-    per = d.slots // parts_kv
-    kv_copies = []
-    for n in range(parts_kv):
-        for which, (src, dst) in enumerate(((kc, kb), (vc, vb))):
-            cp = pltpu.make_async_copy(
-                src.at[pl.ds(n * per, per)], dst.at[pl.ds(n * per, per)], kv_sem.at[which, n]
-            )
-            cp.start()
-            kv_copies.append(cp)
-
     friends = [partner]
     for axis in ("y", "z"):
         for way in (0, 1):
@@ -290,6 +271,15 @@
     barrier = pltpu.get_barrier_semaphore()
     for dev in friends:
         pl.semaphore_signal(barrier, inc=1, device_id=dev, device_id_type=MESH)
+
+    new_copies = [
+        pltpu.make_async_copy(src, dst, io_sem.at[n])
+        for n, (src, dst) in enumerate(((nk_in, nk), (nv_in, nv), (ctx_in, ctx)), 3)
+    ]
+    for cp in new_copies:
+        cp.start()
+    ps_copy = pltpu.make_async_copy(ps, psv, io_sem.at[0])
+    ps_copy.start()
 
     q_copy.wait()
     heads = d.kvl * d.group
@@ -314,6 +304,18 @@
         )
         cp.start()
         waits.append(cp)
+
+    parts_kv = kv_sem.shape[1]
+    per = d.slots // parts_kv
+    kv_copies = []
+    for n in range(parts_kv):
+        for which, (src, dst) in enumerate(((kc, kb), (vc, vb))):
+            cp = pltpu.make_async_copy(
+                src.at[pl.ds(n * per, per)], dst.at[pl.ds(n * per, per)], kv_sem.at[which, n]
+            )
+            cp.start()
+            kv_copies.append(cp)
+
     g[pl.ds(own + tp * d.rd, d.rd)] = qx[tp]
     for k in range(1, d.ntp):
         source = lax.rem(tp - k + d.ntp, d.ntp)

time: 76.2 us -> 76.2 us (level)
  no operation moved by 1% of the time
where the time goes in v8:
time: 76.2 us; the launch traced here: 76 us
  Pallas kernels  75.3 us (99%)
    pallas_call x1, Pallas kernels, shards(): pl.pallas_call(functools.partial(main_kernel, d, order, plan_reduce), out...  75.3 us

profile of v8, /device:TPU:8, one launch (start us, length us, event | category | flops | bytes accessed | tf_op | source)
XLA Modules:
  0.0 76.0 jit_solution(8170788909546873018)
XLA Ops:
  0.0 75.3 %shard_map.73 = bf16[3,2,64,128]{3,2,1,0:T(8,128)(2,1)S(1)} custom-call(s32[512,128]{1,0:T(8,128)} %ps.1, s32[4,128]{1,0:T(4,128)} %bitcast.3, bf16[3,2,8192]{2,1,0:T(2,128)(2,1)} %q_in.1, bf16[3,2,1024]{2,1,0:T(2,128)(2,1)} %nk_in.1, bf16[3,2,1024]{2,1,0:T(2,128)(2,1)} %nv_in.1, bf16[40,256,256]{2,1,0:T(8,128)(2,1)} %kc.1, bf16[40,256,256]{2,1,0:T(8,128)(2,1)} %vc.1), custom_call_target="tpu_custom_call" | custom-call | tf_op jit(solution)/shard_map/pallas_call | solution.py:746
  75.3 0.7 reshape.7

commit v9 on v8

--- a/solution.py
+++ b/solution.py
@@ -392,10 +392,11 @@
     lane_slot = iota((d.q, d.slot_len), 1)
     scale = 1.0 / math.sqrt(HD)
 
-    def attend_many(it, carry):
-        chunk(qs, qp, fw_send, fw_recv, it).wait_recv()
+    batch = 4
+
+    def attend_batch(first, carry):
         m_p, l_p, o_p, mc, lc = carry
-        at = [it * unroll + u for u in range(unroll)]
+        at = [first + u for u in range(batch)]
         rows = [meta[0, i] for i in at]
         q1 = [jnp.where(row >= 0, g[jnp.maximum(row, 0)], qp[i]) for row, i in zip(rows, at)]
         q2 = [jnp.concatenate([q * mask for mask in head_masks], axis=1) for q in q1]
@@ -425,8 +426,14 @@
             lc = jnp.where(lane128 == i, l_p, lc)
         for u, i in enumerate(at):
             o[0, i] = accs[u]
+        return m_p, l_p, o_p, mc, lc
+
+    def attend_many(it, carry):
+        chunk(qs, qp, fw_send, fw_recv, it).wait_recv()
+        for n in range(unroll // batch):
+            carry = attend_batch(it * unroll + n * batch, carry)
         chunk(o.at[0], o.at[1], ex_send, ex_recv, it).start()
-        return m_p, l_p, o_p, mc, lc
+        return carry
 
     zero_col = jnp.zeros((d.q, 1), F32)
     zero = jnp.zeros((d.q, 128), F32)

time: 76.2 us -> 77 us (1.010)
  Pallas kernels: 75.3 us -> 76.1 us
where the time goes in v9:
time: 77 us; the launch traced here: 76.8 us
  Pallas kernels  76.1 us (99%)
    pallas_call x1, Pallas kernels, shards(): pl.pallas_call(functools.partial(main_kernel, d, order, plan_reduce), out...  76.1 us

profile of v9, /device:TPU:8, one launch (start us, length us, event | category | flops | bytes accessed | tf_op | source)
XLA Modules:
  0.0 76.8 jit_solution(5517223705487177182)
XLA Ops:
  0.0 76.1 %shard_map.73 = bf16[3,2,64,128]{3,2,1,0:T(8,128)(2,1)S(1)} custom-call(s32[512,128]{1,0:T(8,128)} %ps.1, s32[4,128]{1,0:T(4,128)} %bitcast.3, bf16[3,2,8192]{2,1,0:T(2,128)(2,1)} %q_in.1, bf16[3,2,1024]{2,1,0:T(2,128)(2,1)} %nk_in.1, bf16[3,2,1024]{2,1,0:T(2,128)(2,1)} %nv_in.1, bf16[40,256,256]{2,1,0:T(8,128)(2,1)} %kc.1, bf16[40,256,256]{2,1,0:T(8,128)(2,1)} %vc.1), custom_call_target="tpu_custom_call" | custom-call | tf_op jit(solution)/shard_map/pallas_call | solution.py:753
  76.1 0.7 reshape.7
